TPU v7x, 32 devices: a whole 2x2x4 slice. The times are simulated.
32 devices in a mesh: gx: 2 (over y), gy: 4 (over z), af: 4 (over x, core).
Axes of the slice: x: 2, y: 2, z: 4, core: 2. Of those that a mesh axis runs over, the one named last changes fastest.
Arguments:
- press_matrix: float32 [8, 16, 2048], P(None, 'gx', ('gy', 'af')), may hold values from -1.5 to 1.5
- cond_matrix: float32 [8, 16, 2048], P(None, 'gx', ('gy', 'af')), may hold values from 0.05 to 0.5
- accum_matrix: float32 [8, 16, 2048], P(None, 'gx', ('gy', 'af')), may hold values from 0.5 to 2
- press_frac: float32 [128, 256], P(('gx', 'gy', 'af')), may hold values from -1.5 to 1.5
- accum_frac: float32 [128, 256], P(('gx', 'gy', 'af')), may hold values from 0.3 to 1
- trans_chain: float32 [128, 256], P(('gx', 'gy', 'af')), may hold values from 0.1 to 1
- couple_mf: float32 [128, 256], P(('gx', 'gy', 'af')), may hold values from 0.7 to 1.4
- couple_fm: float32 [128, 256], P(('gx', 'gy', 'af')), may hold values from 0.6 to 1.2
- conn_tile: int32 [128, 256], P(('gx', 'gy', 'af')), may hold values from 0 to 31, as said below
- conn_layer: int32 [128, 256], P(('gx', 'gy', 'af')), may hold values from 0 to 7
- conn_cell: int32 [128, 256], P(('gx', 'gy', 'af')), may hold values from 0 to 1023
- inter_delta: int32 [128], P(('gx', 'gy', 'af')), may hold values from 0 to 4, as said below
- inter_from: int32 [128], P(('gx', 'gy', 'af')), may hold values from 0 to 255
- inter_to: int32 [128], P(('gx', 'gy', 'af')), may hold values from 0 to 255
- inter_trans: float32 [128], P(('gx', 'gy', 'af')), may hold values from 0.5 to 2
- well_tile: int32 [32], replicated, may hold values from 0 to 31
- well_cell: int32 [32], replicated, may hold values from 0 to 1023
- well_rate: float32 [32], replicated, may hold values from -8 to 8
Outputs:
- res_matrix: float32 [8, 16, 2048], P(None, 'gx', ('gy', 'af'))
- res_fracture: float32 [128, 256], P(('gx', 'gy', 'af'))
- adj_matrix: float32 [8, 16, 2048], P(None, 'gx', ('gy', 'af'))
- adj_fracture: float32 [128, 256], P(('gx', 'gy', 'af'))
Inputs may be any that keep to these rules, and one draw needn't show every extreme that they name: `conn_tile`: in each aligned run of 1024 segments (blocks k * 4 to (k + 1) * 4 - 1), at most 64 segments lie in cells of one tile; in every draw some tile holds exactly 64 segments of every such run. b + inter_delta(b) never passes the last block; the value 4 is reached.
All inputs are finite; a program needn't handle non-finite values.
Results may differ from a plain program's by a relative error of at most 0.00013.
Values sent between devices are 32-bit elements; how exact they have to be, the bound alone decides.
A program may use at most 64 MiB of HBM per device.

v0:
```python
import jax
import jax.numpy as jnp
from jax import lax
from jax.sharding import PartitionSpec as P

ITERS = 8


vertical_factor = 0.5
highest = lax.Precision.HIGHEST


def padded_2(cells, sides, width):
    for axis, dim in sides:
        count = lax.axis_size(axis)
        ends = count - 1
        head = lax.slice_in_dim(cells, 0, width, axis=dim)
        tail = lax.slice_in_dim(cells, cells.shape[dim] - width, cells.shape[dim], axis=dim)
        cells = jnp.concatenate(
            [
                lax.ppermute(tail, axis, [(i, (i + 1) % count) for i in range(ends)]),
                cells,
                lax.ppermute(head, axis, [((i + 1) % count, i) for i in range(ends)]),
            ],
            axis=dim,
        )
    return cells


def passed_along(block, axis, distance):
    devices = range(lax.axis_size(axis))
    route = [(i - distance, i) for i in devices if i - distance in devices]
    return lax.ppermute(block, axis, route)


def harmonic(first, second):
    return 2.0 * first * second / (first + second)


def halo_cells(stacked):
    return padded_2(stacked, (("gx", 2), (("gy", "af"), 3)), 1)


def body(
    press_matrix,
    cond_matrix,
    accum_matrix,
    press_frac,
    accum_frac,
    trans_chain,
    couple_mf,
    couple_fm,
    conn_tile,
    conn_layer,
    conn_cell,
    inter_delta,
    inter_from,
    inter_to,
    inter_trans,
    well_tile,
    well_cell,
    well_rate,
):
    layers, width_x, width_y = press_matrix.shape
    blocks, block_len = press_frac.shape
    segments = blocks * block_len
    tiles = lax.axis_size(("gx", "gy", "af"))
    capacity = 2 * segments // tiles
    my_tile = lax.axis_index(("gx", "gy", "af"))
    padded = halo_cells(jnp.stack([cond_matrix, press_matrix]))
    cond_pad = padded[0]
    press_pad = padded[1]
    trans_x = harmonic(cond_pad[:, :-1, 1:-1], cond_pad[:, 1:, 1:-1])
    trans_y = harmonic(cond_pad[:, 1:-1, :-1], cond_pad[:, 1:-1, 1:])
    trans_z = vertical_factor * harmonic(cond_matrix[:-1], cond_matrix[1:])
    zero_layer = jnp.zeros((1, width_x, width_y), jnp.float32)
    diag_matrix = (
        accum_matrix + trans_x[:, 1:] + trans_x[:, :-1] + trans_y[:, :, 1:] + trans_y[:, :, :-1]
    )
    diag_matrix = (
        diag_matrix
        + jnp.concatenate([trans_z, zero_layer])
        + jnp.concatenate([zero_layer, trans_z])
    )

    def stencil(field_pad, field):
        total = trans_x[:, 1:] * field_pad[:, 2:, 1:-1] + trans_x[:, :-1] * field_pad[:, :-2, 1:-1]
        total = (
            total
            + trans_y[:, :, 1:] * field_pad[:, 1:-1, 2:]
            + trans_y[:, :, :-1] * field_pad[:, 1:-1, :-2]
        )
        total = (
            total
            + jnp.concatenate([trans_z * field[1:], zero_layer])
            + jnp.concatenate([zero_layer, trans_z * field[:-1]])
        )
        return total

    position = jnp.arange(block_len)
    trans_next = jnp.where(position[None, :] < block_len - 1, trans_chain, 0.0)
    zero_col = jnp.zeros((blocks, 1), jnp.float32)
    trans_prev = jnp.concatenate([zero_col, trans_next[:, :-1]], axis=1)
    diag_frac = accum_frac + trans_next + trans_prev + couple_fm

    def chain(field):
        upper = jnp.concatenate([field[:, 1:], zero_col], axis=1)
        lower = jnp.concatenate([zero_col, field[:, :-1]], axis=1)
        return trans_next * upper + trans_prev * lower

    owner = conn_tile.reshape(-1)
    local_cell = conn_layer.reshape(-1) * (width_x * width_y) + conn_cell.reshape(-1)
    seg_ids = jnp.arange(segments, dtype=jnp.int32)
    ranking = jnp.argsort(owner, stable=True)
    sorted_owner = owner[ranking]
    first_seen = jnp.searchsorted(sorted_owner, sorted_owner, side="left")
    bucket_rank = jnp.zeros((segments,), jnp.int32).at[ranking].set(seg_ids - first_seen)
    slot_index = owner * capacity + bucket_rank
    requests = (
        jnp.zeros((tiles * capacity,), jnp.int32)
        .at[slot_index]
        .set(local_cell)
        .reshape(tiles, capacity)
    )
    wanted = lax.all_to_all(
        requests, ("gx", "gy", "af"), split_axis=0, concat_axis=0, tiled=True
    ).reshape(-1)
    owner_hot = (owner[:, None] == jnp.arange(tiles, dtype=jnp.int32)[None, :]).astype(jnp.float32)
    rank_hot = (bucket_rank[:, None] == jnp.arange(capacity, dtype=jnp.int32)[None, :]).astype(
        jnp.float32
    )
    cell_row = wanted // width_y
    cell_col = wanted % width_y
    row_hot = (cell_row[:, None] == jnp.arange(layers * width_x, dtype=jnp.int32)[None, :]).astype(
        jnp.float32
    )
    col_hot = (cell_col[:, None] == jnp.arange(width_y, dtype=jnp.int32)[None, :]).astype(
        jnp.float32
    )

    def cross(field_matrix, send_frac):
        rows_picked = jnp.dot(
            row_hot,
            field_matrix.reshape(layers * width_x, width_y),
            precision=highest,
            preferred_element_type=jnp.float32,
        )
        values = jnp.sum(rows_picked * col_hot, axis=1).reshape(tiles, capacity)
        weighted = send_frac.reshape(-1)[:, None] * rank_hot
        outgoing = lax.dot_general(
            owner_hot,
            weighted,
            (((0,), (0,)), ((), ())),
            precision=highest,
            preferred_element_type=jnp.float32,
        )
        back_values, incoming = (
            lax.all_to_all(values, ("gx", "gy", "af"), split_axis=0, concat_axis=0, tiled=True),
            lax.all_to_all(outgoing, ("gx", "gy", "af"), split_axis=0, concat_axis=0, tiled=True),
        )
        owner_rows = jnp.dot(
            owner_hot, back_values, precision=highest, preferred_element_type=jnp.float32
        )
        seg_values = jnp.sum(owner_rows * rank_hot, axis=1).reshape(blocks, block_len)
        spread = incoming.reshape(-1)[:, None] * col_hot
        cell_sum = lax.dot_general(
            row_hot,
            spread,
            (((0,), (0,)), ((), ())),
            precision=highest,
            preferred_element_type=jnp.float32,
        )
        return (cell_sum.reshape(layers, width_x, width_y), seg_values)

    partner_row = jnp.arange(blocks, dtype=jnp.int32) + inter_delta
    from_hot = (position[None, :] == inter_from[:, None]).astype(jnp.float32)
    mine = jnp.where(well_tile == my_tile, well_rate, 0.0)
    source_flat = jnp.zeros((width_x * width_y,), jnp.float32).at[well_cell].add(mine)
    source = jnp.broadcast_to(source_flat.reshape(1, width_x, width_y), (layers, width_x, width_y))
    cell_sum, seg_values = cross(press_matrix, couple_mf * press_frac)
    res_matrix = diag_matrix * press_matrix - stencil(press_pad, press_matrix) - cell_sum - source
    following = passed_along(press_frac, ("gx", "gy", "af"), -1)
    joined = jnp.concatenate([press_frac, following], axis=0)
    picked = joined[partner_row, inter_to]
    res_fracture = (
        diag_frac * press_frac
        - chain(press_frac)
        - couple_fm * seg_values
        - from_hot * (inter_trans * picked)[:, None]
    )
    adj_matrix = res_matrix / diag_matrix
    adj_fracture = res_fracture / diag_frac
    for sweep_index in range(ITERS - 1):
        field_pad = halo_cells(adj_matrix[None])[0]
        cell_sum, seg_values = cross(adj_matrix, couple_fm * adj_fracture)
        image_matrix = diag_matrix * adj_matrix - stencil(field_pad, adj_matrix) - cell_sum
        adjoint_picked = inter_trans * jnp.sum(from_hot * adj_fracture, axis=1)
        adjoint_spread = (
            jnp.zeros((2 * blocks, block_len), jnp.float32)
            .at[partner_row, inter_to]
            .add(adjoint_picked)
        )
        arrived = passed_along(adjoint_spread[blocks:], ("gx", "gy", "af"), 1)
        image_fracture = (
            diag_frac * adj_fracture
            - chain(adj_fracture)
            - couple_mf * seg_values
            - (adjoint_spread[:blocks] + arrived)
        )
        adj_matrix = adj_matrix + (res_matrix - image_matrix) / diag_matrix
        adj_fracture = adj_fracture + (res_fracture - image_fracture) / diag_frac
    return (res_matrix, res_fracture, adj_matrix, adj_fracture)


def solution(mesh):
    in_specs = (
        P(None, "gx", ("gy", "af")),
        P(None, "gx", ("gy", "af")),
        P(None, "gx", ("gy", "af")),
        P(("gx", "gy", "af"), None),
        P(("gx", "gy", "af"), None),
        P(("gx", "gy", "af"), None),
        P(("gx", "gy", "af"), None),
        P(("gx", "gy", "af"), None),
        P(("gx", "gy", "af"), None),
        P(("gx", "gy", "af"), None),
        P(("gx", "gy", "af"), None),
        P(("gx", "gy", "af")),
        P(("gx", "gy", "af")),
        P(("gx", "gy", "af")),
        P(("gx", "gy", "af")),
        P(),
        P(),
        P(),
    )
    out_specs = (
        P(None, "gx", ("gy", "af")),
        P(("gx", "gy", "af"), None),
        P(None, "gx", ("gy", "af")),
        P(("gx", "gy", "af"), None),
    )
    return jax.shard_map(body, mesh=mesh, in_specs=in_specs, out_specs=out_specs, check_vma=False)
```

profile of v0, /device:TPU:0, one launch (start us, length us, event | category | flops | bytes accessed | tf_op | source)
XLA Modules:
  0.0 395.1 jit_solution(12885213983922734106)
XLA Ops:
  10.2 50.7 %while.25 = (s32[]{:T(128)}, u32[1024]{0:T(1024)S(1)}, u32[1024]{0:T(1024)S(1)}, s32[1024]{0:T(1024)S(1)}, s32[]{:T(128)}, /*index=5*/s32[]{:T(128)}, s32[]{}) while((s32[]{:T(128)}, u32[1024]{0:T(1024)S(1)}, u32[1024]{0:T(1024)S(1)}, s32[1024]{0:T(1024)S(1)}, s32[]{:T(128)}, /*index=5*/s32[]{:T(128)}, s32[]{}) %tuple.94), condition=%wide.region_2.3_spmd.clone, body=%wide.region_1.2_spmd.clone.sunk | while | flops 19460 | bytes 67685 | solution.py:116
  10.3 4.5 %gather_fusion = s32[1024]{0:T(1024)S(1)} fusion(s32[1024]{0:T(1024)S(1)} %get-tuple-element.244, u32[1024]{0:T(1024)S(1)} %broadcast_clamp_fusion.3), kind=kCustom, calls=%fused_computation.clone.clone.1 | custom fusion | bytes 12288 | tf_op jit(solution)/shard_map/jit(searchsorted)/jit(_searchsorted_scan_impl)/vmap(jit(_searchsorted_scan_impl))/while/body/eval_jaxpr/gather | solution.py:116
  14.9 4.5 %gather_fusion = s32[1024]{0:T(1024)S(1)} fusion(s32[1024]{0:T(1024)S(1)} %get-tuple-element.244, u32[1024]{0:T(1024)S(1)} %broadcast_clamp_fusion.3), kind=kCustom, calls=%fused_computation.clone.clone.1 | custom fusion | bytes 12288 | tf_op jit(solution)/shard_map/jit(searchsorted)/jit(_searchsorted_scan_impl)/vmap(jit(_searchsorted_scan_impl))/while/body/eval_jaxpr/gather | solution.py:116
  19.5 4.5 %gather_fusion = s32[1024]{0:T(1024)S(1)} fusion(s32[1024]{0:T(1024)S(1)} %get-tuple-element.244, u32[1024]{0:T(1024)S(1)} %broadcast_clamp_fusion.3), kind=kCustom, calls=%fused_computation.clone.clone.1 | custom fusion | bytes 12288 | tf_op jit(solution)/shard_map/jit(searchsorted)/jit(_searchsorted_scan_impl)/vmap(jit(_searchsorted_scan_impl))/while/body/eval_jaxpr/gather | solution.py:116
  24.1 4.5 %gather_fusion = s32[1024]{0:T(1024)S(1)} fusion(s32[1024]{0:T(1024)S(1)} %get-tuple-element.244, u32[1024]{0:T(1024)S(1)} %broadcast_clamp_fusion.3), kind=kCustom, calls=%fused_computation.clone.clone.1 | custom fusion | bytes 12288 | tf_op jit(solution)/shard_map/jit(searchsorted)/jit(_searchsorted_scan_impl)/vmap(jit(_searchsorted_scan_impl))/while/body/eval_jaxpr/gather | solution.py:116
  33.3 4.5 %gather_fusion = s32[1024]{0:T(1024)S(1)} fusion(s32[1024]{0:T(1024)S(1)} %get-tuple-element.244, u32[1024]{0:T(1024)S(1)} %broadcast_clamp_fusion.3), kind=kCustom, calls=%fused_computation.clone.clone.1 | custom fusion | bytes 12288 | tf_op jit(solution)/shard_map/jit(searchsorted)/jit(_searchsorted_scan_impl)/vmap(jit(_searchsorted_scan_impl))/while/body/eval_jaxpr/gather | solution.py:116
  71.1 7.3 %all-to-all-start = ((s32[32,1,64]{2,1,0:T(1,128)}), s32[32,1,64]{2,1,0:T(1,128)S(1)}, u32[]{:S(2)}, u32[]{:S(2)}) async-start(s32[32,1,64]{2,1,0:T(1,128)} %all_to_all.118), calls=%async_computation | async-start | bytes 32768 | tf_op jit(solution)/shard_map/all_to_all | solution.py:125
  79.7 8.3 %collective-permute-start = (f32[2,8,1,128]{3,2,1,0:T(1,128)S(1)}, f32[2,8,1,128]{3,2,1,0:T(1,128)S(1)}, u32[]{:S(2)}, u32[]{:S(2)}) collective-permute-start(f32[2,8,1,128]{3,2,1,0:T(1,128)S(1)} %get-tuple-element.135), channel_id=1, source_target_pairs={{0,16},{1,17},{2,18},{3,19},{4,20},{5,21},{6,22},{7,23},{8,24},{9,... | collective-permute-start | bytes 24584 | tf_op jit(solution)/shard_map/ppermute | solution.py:21
  101.9 8.1 %all-to-all-start.2 = ((f32[32,1,64]{2,1,0:T(1,128)}), f32[32,1,64]{2,1,0:T(1,128)S(1)}, u32[]{:S(2)}, u32[]{:S(2)}) async-start(f32[32,1,64]{2,1,0:T(1,128)} %all_to_all.122), calls=%async_computation.2 | async-start | bytes 32768 | tf_op jit(solution)/shard_map/all_to_all | solution.py:158
  110.1 7.0 %all-to-all-done.2 = f32[32,1,64]{2,1,0:T(1,128)S(1)} async-done(((f32[32,1,64]{2,1,0:T(1,128)}), f32[32,1,64]{2,1,0:T(1,128)S(1)}, u32[]{:S(2)}, u32[]{:S(2)}) %all-to-all-start.2) | async-done | bytes 8224 | tf_op jit(solution)/shard_map/all_to_all | solution.py:158
  144.7 4.8 %all-to-all-start.4 = ((f32[32,1,64]{2,1,0:T(1,128)}), f32[32,1,64]{2,1,0:T(1,128)S(1)}, u32[]{:S(2)}, u32[]{:S(2)}) async-start(f32[32,1,64]{2,1,0:T(1,128)} %all_to_all.127), calls=%async_computation.4 | async-start | bytes 32768 | tf_op jit(solution)/shard_map/all_to_all | solution.py:158
  149.7 6.9 %all-to-all-done.4 = f32[32,1,64]{2,1,0:T(1,128)S(1)} async-done(((f32[32,1,64]{2,1,0:T(1,128)}), f32[32,1,64]{2,1,0:T(1,128)S(1)}, u32[]{:S(2)}, u32[]{:S(2)}) %all-to-all-start.4) | async-done | bytes 8224 | tf_op jit(solution)/shard_map/all_to_all | solution.py:158
  171.5 4.5 %collective-permute-start.9 = (f32[1,8,1,128]{3,2,1,0:T(1,128)S(1)}, f32[1,8,1,128]{3,2,1,0:T(1,128)S(1)}, u32[]{:S(2)}, u32[]{:S(2)}) collective-permute-start(f32[1,8,1,128]{3,2,1,0:T(1,128)S(1)} %get-tuple-element.161), channel_id=1, source_target_pairs={{0,16},{1,17},{2,18},{3,19},{4,20},{5,21},{6,22},{7,23},{8,24},{9,... | collective-permute-start | bytes 12296 | tf_op jit(solution)/shard_map/ppermute | solution.py:21
  182.1 6.5 %all-to-all-start.6 = ((f32[32,1,64]{2,1,0:T(1,128)}), f32[32,1,64]{2,1,0:T(1,128)S(1)}, u32[]{:S(2)}, u32[]{:S(2)}) async-start(f32[32,1,64]{2,1,0:T(1,128)} %all_to_all.132), calls=%async_computation.6 | async-start | bytes 32768 | tf_op jit(solution)/shard_map/all_to_all | solution.py:158
  188.9 6.9 %all-to-all-done.6 = f32[32,1,64]{2,1,0:T(1,128)S(1)} async-done(((f32[32,1,64]{2,1,0:T(1,128)}), f32[32,1,64]{2,1,0:T(1,128)S(1)}, u32[]{:S(2)}, u32[]{:S(2)}) %all-to-all-start.6) | async-done | bytes 8224 | tf_op jit(solution)/shard_map/all_to_all | solution.py:158
  222.0 4.8 %all-to-all-start.8 = ((f32[32,1,64]{2,1,0:T(1,128)}), f32[32,1,64]{2,1,0:T(1,128)S(1)}, u32[]{:S(2)}, u32[]{:S(2)}) async-start(f32[32,1,64]{2,1,0:T(1,128)} %all_to_all.137), calls=%async_computation.8 | async-start | bytes 32768 | tf_op jit(solution)/shard_map/all_to_all | solution.py:158
  227.0 6.9 %all-to-all-done.8 = f32[32,1,64]{2,1,0:T(1,128)S(1)} async-done(((f32[32,1,64]{2,1,0:T(1,128)}), f32[32,1,64]{2,1,0:T(1,128)S(1)}, u32[]{:S(2)}, u32[]{:S(2)}) %all-to-all-start.8) | async-done | bytes 8224 | tf_op jit(solution)/shard_map/all_to_all | solution.py:158
  260.1 4.8 %all-to-all-start.10 = ((f32[32,1,64]{2,1,0:T(1,128)}), f32[32,1,64]{2,1,0:T(1,128)S(1)}, u32[]{:S(2)}, u32[]{:S(2)}) async-start(f32[32,1,64]{2,1,0:T(1,128)} %all_to_all.142), calls=%async_computation.10 | async-start | bytes 32768 | tf_op jit(solution)/shard_map/all_to_all | solution.py:158
  265.1 6.9 %all-to-all-done.10 = f32[32,1,64]{2,1,0:T(1,128)S(1)} async-done(((f32[32,1,64]{2,1,0:T(1,128)}), f32[32,1,64]{2,1,0:T(1,128)S(1)}, u32[]{:S(2)}, u32[]{:S(2)}) %all-to-all-start.10) | async-done | bytes 8224 | tf_op jit(solution)/shard_map/all_to_all | solution.py:158
  298.3 5.0 %all-to-all-start.12 = ((f32[32,1,64]{2,1,0:T(1,128)}), f32[32,1,64]{2,1,0:T(1,128)S(1)}, u32[]{:S(2)}, u32[]{:S(2)}) async-start(f32[32,1,64]{2,1,0:T(1,128)} %all_to_all.147), calls=%async_computation.12 | async-start | bytes 32768 | tf_op jit(solution)/shard_map/all_to_all | solution.py:158
  303.5 6.7 %all-to-all-done.12 = f32[32,1,64]{2,1,0:T(1,128)S(1)} async-done(((f32[32,1,64]{2,1,0:T(1,128)}), f32[32,1,64]{2,1,0:T(1,128)S(1)}, u32[]{:S(2)}, u32[]{:S(2)}) %all-to-all-start.12) | async-done | bytes 8224 | tf_op jit(solution)/shard_map/all_to_all | solution.py:158
  336.4 4.8 %all-to-all-start.14 = ((f32[32,1,64]{2,1,0:T(1,128)}), f32[32,1,64]{2,1,0:T(1,128)S(1)}, u32[]{:S(2)}, u32[]{:S(2)}) async-start(f32[32,1,64]{2,1,0:T(1,128)} %all_to_all.152), calls=%async_computation.14 | async-start | bytes 32768 | tf_op jit(solution)/shard_map/all_to_all | solution.py:158
  341.4 6.9 %all-to-all-done.14 = f32[32,1,64]{2,1,0:T(1,128)S(1)} async-done(((f32[32,1,64]{2,1,0:T(1,128)}), f32[32,1,64]{2,1,0:T(1,128)S(1)}, u32[]{:S(2)}, u32[]{:S(2)}) %all-to-all-start.14) | async-done | bytes 8224 | tf_op jit(solution)/shard_map/all_to_all | solution.py:158
  385.6 6.9 %all-to-all-done.15 = f32[32,1,64]{2,1,0:T(1,128)S(1)} async-done(((f32[32,1,64]{2,1,0:T(1,128)}), f32[32,1,64]{2,1,0:T(1,128)S(1)}, u32[]{:S(2)}, u32[]{:S(2)}) %all-to-all-start.15) | async-done | bytes 8224 | tf_op jit(solution)/shard_map/all_to_all | solution.py:159
  (375 shorter events, 255.5 us)
Async XLA Ops:
  71.1 27.6 %all-to-all-start = ((s32[32,1,64]{2,1,0:T(1,128)}), s32[32,1,64]{2,1,0:T(1,128)S(1)}, u32[]{:S(2)}, u32[]{:S(2)}) async-start(s32[32,1,64]{2,1,0:T(1,128)} %all_to_all.118), calls=%async_computation | async-start | bytes 32768 | tf_op jit(solution)/shard_map/all_to_all | solution.py:125
  78.4 17.9 %collective-permute-start.4 = (f32[4,256]{1,0:T(4,128)S(1)}, f32[4,256]{1,0:T(4,128)S(1)}, u32[]{:S(2)}, u32[]{:S(2)}) collective-permute-start(f32[4,256]{1,0:T(4,128)S(1)} %copy-done.6), channel_id=1, source_target_pairs={{1,0},{2,1},{3,2},{4,3},{5,4},{6,5},{7,6},{8,7},{9,8},{10,9},{11,1... | collective-permute-start | bytes 12296 | tf_op jit(solution)/shard_map/ppermute | solution.py:33
  79.7 13.2 %collective-permute-start = (f32[2,8,1,128]{3,2,1,0:T(1,128)S(1)}, f32[2,8,1,128]{3,2,1,0:T(1,128)S(1)}, u32[]{:S(2)}, u32[]{:S(2)}) collective-permute-start(f32[2,8,1,128]{3,2,1,0:T(1,128)S(1)} %get-tuple-element.135), channel_id=1, source_target_pairs={{0,16},{1,17},{2,18},{3,19},{4,20},{5,21},{6,22},{7,23},{8,24},{9,... | collective-permute-start | bytes 24584 | tf_op jit(solution)/shard_map/ppermute | solution.py:21
  101.9 15.2 %all-to-all-start.2 = ((f32[32,1,64]{2,1,0:T(1,128)}), f32[32,1,64]{2,1,0:T(1,128)S(1)}, u32[]{:S(2)}, u32[]{:S(2)}) async-start(f32[32,1,64]{2,1,0:T(1,128)} %all_to_all.122), calls=%async_computation.2 | async-start | bytes 32768 | tf_op jit(solution)/shard_map/all_to_all | solution.py:158
  119.8 9.6 %all-to-all-start.1 = ((f32[32,1,64]{2,1,0:T(1,128)}), f32[32,1,64]{2,1,0:T(1,128)S(1)}, u32[]{:S(2)}, u32[]{:S(2)}) async-start(f32[32,1,64]{2,1,0:T(1,128)} %bitcast.5), calls=%async_computation.1 | async-start | bytes 32768 | tf_op jit(solution)/shard_map/all_to_all | solution.py:159
  123.1 34.0 %collective-permute-start.13 = (f32[4,256]{1,0:T(4,128)S(1)}, f32[4,256]{1,0:T(4,128)S(1)}, u32[]{:S(2)}, u32[]{:S(2)}) collective-permute-start(f32[4,256]{1,0:T(4,128)S(1)} %slice.584), channel_id=1, source_target_pairs={{0,1},{1,2},{2,3},{3,4},{4,5},{5,6},{6,7},{7,8},{8,9},{9,10},{10,1... | collective-permute-start | bytes 12296 | tf_op jit(solution)/shard_map/ppermute | solution.py:33
  144.7 11.9 %all-to-all-start.4 = ((f32[32,1,64]{2,1,0:T(1,128)}), f32[32,1,64]{2,1,0:T(1,128)S(1)}, u32[]{:S(2)}, u32[]{:S(2)}) async-start(f32[32,1,64]{2,1,0:T(1,128)} %all_to_all.127), calls=%async_computation.4 | async-start | bytes 32768 | tf_op jit(solution)/shard_map/all_to_all | solution.py:158
  161.9 34.5 %collective-permute-start.18 = (f32[4,256]{1,0:T(4,128)S(1)}, f32[4,256]{1,0:T(4,128)S(1)}, u32[]{:S(2)}, u32[]{:S(2)}) collective-permute-start(f32[4,256]{1,0:T(4,128)S(1)} %slice.598), channel_id=1, source_target_pairs={{0,1},{1,2},{2,3},{3,4},{4,5},{5,6},{6,7},{7,8},{8,9},{9,10},{10,1... | collective-permute-start | bytes 12296 | tf_op jit(solution)/shard_map/ppermute | solution.py:33
  177.4 11.2 %collective-permute-start.11 = (f32[1,8,10,1]{3,2,1,0:T(8,128)S(1)}, f32[1,8,10,1]{3,2,1,0:T(8,128)S(1)}, u32[]{:S(2)}, u32[]{:S(2)}) collective-permute-start(f32[1,8,10,1]{3,2,1,0:T(8,128)S(1)} %get-tuple-element.131), channel_id=1, source_target_pairs={{0,1},{1,2},{2,3},{3,4},{4,5},{5,6},{6,7},{7,8},{8,9},{9,10},{10,1... | collective-permute-start | bytes 968 | tf_op jit(solution)/shard_map/ppermute | solution.py:21
  178.7 9.9 %collective-permute-start.12 = (f32[1,8,10,1]{3,2,1,0:T(8,128)S(1)}, f32[1,8,10,1]{3,2,1,0:T(8,128)S(1)}, u32[]{:S(2)}, u32[]{:S(2)}) collective-permute-start(f32[1,8,10,1]{3,2,1,0:T(8,128)S(1)} %get-tuple-element.132), channel_id=1, source_target_pairs={{1,0},{2,1},{3,2},{4,3},{5,4},{6,5},{7,6},{8,7},{9,8},{10,9},{11,1... | collective-permute-start | bytes 968 | tf_op jit(solution)/shard_map/ppermute | solution.py:23
  182.1 13.6 %all-to-all-start.6 = ((f32[32,1,64]{2,1,0:T(1,128)}), f32[32,1,64]{2,1,0:T(1,128)S(1)}, u32[]{:S(2)}, u32[]{:S(2)}) async-start(f32[32,1,64]{2,1,0:T(1,128)} %all_to_all.132), calls=%async_computation.6 | async-start | bytes 32768 | tf_op jit(solution)/shard_map/all_to_all | solution.py:158
  201.0 33.4 %collective-permute-start.23 = (f32[4,256]{1,0:T(4,128)S(1)}, f32[4,256]{1,0:T(4,128)S(1)}, u32[]{:S(2)}, u32[]{:S(2)}) collective-permute-start(f32[4,256]{1,0:T(4,128)S(1)} %slice.612), channel_id=1, source_target_pairs={{0,1},{1,2},{2,3},{3,4},{4,5},{5,6},{6,7},{7,8},{8,9},{9,10},{10,1... | collective-permute-start | bytes 12296 | tf_op jit(solution)/shard_map/ppermute | solution.py:33
  222.0 11.9 %all-to-all-start.8 = ((f32[32,1,64]{2,1,0:T(1,128)}), f32[32,1,64]{2,1,0:T(1,128)S(1)}, u32[]{:S(2)}, u32[]{:S(2)}) async-start(f32[32,1,64]{2,1,0:T(1,128)} %all_to_all.137), calls=%async_computation.8 | async-start | bytes 32768 | tf_op jit(solution)/shard_map/all_to_all | solution.py:158
  239.2 33.4 %collective-permute-start.28 = (f32[4,256]{1,0:T(4,128)S(1)}, f32[4,256]{1,0:T(4,128)S(1)}, u32[]{:S(2)}, u32[]{:S(2)}) collective-permute-start(f32[4,256]{1,0:T(4,128)S(1)} %slice.626), channel_id=1, source_target_pairs={{0,1},{1,2},{2,3},{3,4},{4,5},{5,6},{6,7},{7,8},{8,9},{9,10},{10,1... | collective-permute-start | bytes 12296 | tf_op jit(solution)/shard_map/ppermute | solution.py:33
  260.1 11.9 %all-to-all-start.10 = ((f32[32,1,64]{2,1,0:T(1,128)}), f32[32,1,64]{2,1,0:T(1,128)S(1)}, u32[]{:S(2)}, u32[]{:S(2)}) async-start(f32[32,1,64]{2,1,0:T(1,128)} %all_to_all.142), calls=%async_computation.10 | async-start | bytes 32768 | tf_op jit(solution)/shard_map/all_to_all | solution.py:158
  277.3 33.4 %collective-permute-start.33 = (f32[4,256]{1,0:T(4,128)S(1)}, f32[4,256]{1,0:T(4,128)S(1)}, u32[]{:S(2)}, u32[]{:S(2)}) collective-permute-start(f32[4,256]{1,0:T(4,128)S(1)} %slice.640), channel_id=1, source_target_pairs={{0,1},{1,2},{2,3},{3,4},{4,5},{5,6},{6,7},{7,8},{8,9},{9,10},{10,1... | collective-permute-start | bytes 12296 | tf_op jit(solution)/shard_map/ppermute | solution.py:33
  298.3 11.9 %all-to-all-start.12 = ((f32[32,1,64]{2,1,0:T(1,128)}), f32[32,1,64]{2,1,0:T(1,128)S(1)}, u32[]{:S(2)}, u32[]{:S(2)}) async-start(f32[32,1,64]{2,1,0:T(1,128)} %all_to_all.147), calls=%async_computation.12 | async-start | bytes 32768 | tf_op jit(solution)/shard_map/all_to_all | solution.py:158
  315.5 33.4 %collective-permute-start.38 = (f32[4,256]{1,0:T(4,128)S(1)}, f32[4,256]{1,0:T(4,128)S(1)}, u32[]{:S(2)}, u32[]{:S(2)}) collective-permute-start(f32[4,256]{1,0:T(4,128)S(1)} %slice.654), channel_id=1, source_target_pairs={{0,1},{1,2},{2,3},{3,4},{4,5},{5,6},{6,7},{7,8},{8,9},{9,10},{10,1... | collective-permute-start | bytes 12296 | tf_op jit(solution)/shard_map/ppermute | solution.py:33
  336.4 11.9 %all-to-all-start.14 = ((f32[32,1,64]{2,1,0:T(1,128)}), f32[32,1,64]{2,1,0:T(1,128)S(1)}, u32[]{:S(2)}, u32[]{:S(2)}) async-start(f32[32,1,64]{2,1,0:T(1,128)} %all_to_all.152), calls=%async_computation.14 | async-start | bytes 32768 | tf_op jit(solution)/shard_map/all_to_all | solution.py:158
  353.6 25.4 %collective-permute-start.39 = (f32[4,256]{1,0:T(4,128)S(1)}, f32[4,256]{1,0:T(4,128)S(1)}, u32[]{:S(2)}, u32[]{:S(2)}) collective-permute-start(f32[4,256]{1,0:T(4,128)S(1)} %slice.658), channel_id=1, source_target_pairs={{0,1},{1,2},{2,3},{3,4},{4,5},{5,6},{6,7},{7,8},{8,9},{9,10},{10,1... | collective-permute-start | bytes 12296 | tf_op jit(solution)/shard_map/ppermute | solution.py:33
  367.7 10.8 %all-to-all-start.16 = ((f32[32,1,64]{2,1,0:T(1,128)}), f32[32,1,64]{2,1,0:T(1,128)S(1)}, u32[]{:S(2)}, u32[]{:S(2)}) async-start(f32[32,1,64]{2,1,0:T(1,128)} %all_to_all.157), calls=%async_computation.16 | async-start | bytes 32768 | tf_op jit(solution)/shard_map/all_to_all | solution.py:158
  371.5 13.9 %collective-permute-start.36 = (f32[1,8,10,1]{3,2,1,0:T(8,128)S(1)}, f32[1,8,10,1]{3,2,1,0:T(8,128)S(1)}, u32[]{:S(2)}, u32[]{:S(2)}) collective-permute-start(f32[1,8,10,1]{3,2,1,0:T(8,128)S(1)} %get-tuple-element.121), channel_id=1, source_target_pairs={{0,1},{1,2},{2,3},{3,4},{4,5},{5,6},{6,7},{7,8},{8,9},{9,10},{10,1... | collective-permute-start | bytes 968 | tf_op jit(solution)/shard_map/ppermute | solution.py:21
  373.7 11.8 %collective-permute-start.37 = (f32[1,8,10,1]{3,2,1,0:T(8,128)S(1)}, f32[1,8,10,1]{3,2,1,0:T(8,128)S(1)}, u32[]{:S(2)}, u32[]{:S(2)}) collective-permute-start(f32[1,8,10,1]{3,2,1,0:T(8,128)S(1)} %get-tuple-element.122), channel_id=1, source_target_pairs={{1,0},{2,1},{3,2},{4,3},{5,4},{6,5},{7,6},{8,7},{9,8},{10,9},{11,1... | collective-permute-start | bytes 968 | tf_op jit(solution)/shard_map/ppermute | solution.py:23
  381.0 11.6 %all-to-all-start.15 = ((f32[32,1,64]{2,1,0:T(1,128)}), f32[32,1,64]{2,1,0:T(1,128)S(1)}, u32[]{:S(2)}, u32[]{:S(2)}) async-start(f32[32,1,64]{2,1,0:T(1,128)} %bitcast.59), calls=%async_computation.15 | async-start | bytes 32768 | tf_op jit(solution)/shard_map/all_to_all | solution.py:159
  (53 other events, 863.1 us)
where the time goes:
time: 397 us; the launch traced here: 395 us
  starting transfers between devices  147 us (37%)
  waiting for transfers between devices  112 us (28%)
  local copies, waits for them, and re-layouts  77.7 us (20%)
  matrix products  34.5 us (9%)
  other arithmetic  20.3 us (5%)
    all_to_all x8, waiting for transfers between devices, cross(): lax.all_to_all(values, ('gx', 'gy', 'af'), split_axis=0, concat_axis=0, t...  51.6 us
    gather x11, local copies, waits for them, and re-layouts, body(): first_seen = jnp.searchsorted(sorted_owner, sorted_owner, side='left')  49.8 us
    all_to_all x8, starting transfers between devices, cross(): lax.all_to_all(values, ('gx', 'gy', 'af'), split_axis=0, concat_axis=0, t...  42.6 us
    ppermute x16, starting transfers between devices, padded_2(): lax.ppermute(tail, axis, [(i, (i + 1) % count) for i in range(ends)])  39 us
    all_to_all x8, waiting for transfers between devices, cross(): lax.all_to_all(outgoing, ('gx', 'gy', 'af'), split_axis=0, concat_axis=0,...  36.6 us
    ppermute x16, waiting for transfers between devices, padded_2(): lax.ppermute(head, axis, [((i + 1) % count, i) for i in range(ends)])  22.8 us
    all_to_all x8, starting transfers between devices, cross(): lax.all_to_all(outgoing, ('gx', 'gy', 'af'), split_axis=0, concat_axis=0,...  22.3 us
    ppermute x16, starting transfers between devices, padded_2(): lax.ppermute(head, axis, [((i + 1) % count, i) for i in range(ends)])  20.9 us
  transfers between devices with their start and end apart: 57, of which 24 were waited for; matrix products, arithmetic and copies ran while one was open for 10% of the time, Pallas kernels for 0%

commit v1 on v0

v1 whole, which is shorter than its diff:
```python
import functools

import jax
import jax.numpy as jnp
from jax import lax
from jax.experimental import pallas as pl
from jax.experimental.pallas import tpu as pltpu
from jax.sharding import PartitionSpec as P

ITERS = 8
ROUNDS = ITERS + 1
SLOT = 64
MESH = pl.DeviceIdType.MESH
f32 = jnp.float32
bf16 = jnp.bfloat16


def harmonic(first, second):
    return 2.0 * first * second / (first + second)


def iota(shape, dim):
    return lax.broadcasted_iota(jnp.int32, shape, dim)


def hot(mask):
    return jnp.where(mask, 1.0, 0.0)


def pieces(values):
    high = values.astype(bf16)
    return high, (values - high.astype(f32)).astype(bf16)


def dot_nn(a, b):
    return lax.dot_general(a, b, (((1,), (0,)), ((), ())), preferred_element_type=f32)


def dot_nt(a, b):
    return lax.dot_general(a, b, (((1,), (1,)), ((), ())), preferred_element_type=f32)


def pick(table, lanes_twice, rows):
    found = dot_nn(jnp.concatenate(pieces(table), axis=1), lanes_twice)
    return jnp.sum(found * rows, axis=0, keepdims=True)


def spread(values, rows, lanes):
    count = rows.shape[0]
    both = dot_nt(jnp.concatenate(pieces(rows * values), axis=0), lanes)
    return both[:count] + both[count:]


def kernel(
    sizes,
    press_ref,
    cond_ref,
    accum_ref,
    pfrac_ref,
    afrac_ref,
    chain_ref,
    mf_ref,
    fm_ref,
    tile_ref,
    layer_ref,
    cell_ref,
    delta_ref,
    from_ref,
    to_ref,
    itrans_ref,
    wtile_ref,
    wcell_ref,
    wrate_ref,
    resm_ref,
    resf_ref,
    adjm_ref,
    adjf_ref,
    trans_ref,
    invm_ref,
    frac_ref,
    inter_ref,
    cols_ref,
    rows_ref,
    owner_ref,
    rankv_ref,
    ranko_ref,
    send_ref,
    recv_ref,
    hsend_ref,
    hrecv_ref,
    next_ref,
    send_sem,
    recv_sem,
    hsend_sem,
    hrecv_sem,
    next_sem,
):
    n_gx, n_gy, n_af = sizes
    tiles = n_gx * n_gy * n_af
    half = tiles // 2
    layers, width_x, width_y = press_ref.shape
    blocks, block_len = pfrac_ref.shape
    segments = blocks * block_len
    gx, gy, af = lax.axis_index("gx"), lax.axis_index("gy"), lax.axis_index("af")
    me = (gx * n_gy + gy) * n_af + af

    def place(t):
        return (t // (n_gy * n_af), (t // n_af) % n_gy, t % n_af)

    barrier = pltpu.get_barrier_semaphore()

    def greet(k, carry):
        pl.semaphore_signal(
            barrier, inc=1, device_id=place(lax.rem(me + k, tiles)), device_id_type=MESH
        )
        return carry

    lax.fori_loop(1, tiles, greet, 0)

    lane = iota((8, 128), 1)
    sub = iota((8, 128), 0)
    lane_t = iota((tiles, 128), 1)
    row_t = iota((tiles, 128), 0)
    lane_h = iota((half, 128), 1)
    left_half = lane_h < SLOT

    def flat(x):
        return jnp.concatenate([x[b : b + 1, :] for b in range(blocks)], axis=1)

    def folded(v):
        rows = [v[:, b * block_len : (b + 1) * block_len] for b in range(blocks)]
        return jnp.concatenate(rows + [jnp.zeros((8 - blocks, block_len), f32)], axis=0)

    def padded(ref):
        x = ref[...]
        return jnp.concatenate([x, jnp.zeros((8 - blocks, block_len), x.dtype)], axis=0)

    def packed_lanes(x):
        return jnp.concatenate([x[j : j + 1, :] for j in range(half)], axis=1)

    halo_to = (
        place(lax.rem(me + tiles - 1, tiles)),
        place(lax.rem(me + 1, tiles)),
        (lax.rem(gx + n_gx - 1, n_gx), gy, af),
        (lax.rem(gx + 1, n_gx), gy, af),
    )

    def halo_copy(r, side):
        return pltpu.make_async_remote_copy(
            src_ref=hsend_ref.at[r, side],
            dst_ref=hrecv_ref.at[r, side],
            send_sem=hsend_sem.at[r, side],
            recv_sem=hrecv_sem.at[r, side],
            device_id=halo_to[side],
            device_id_type=MESH,
        )

    def put_halo(r, field, extra):
        low = jnp.zeros((8, 128), f32)
        high = extra
        for z in range(layers):
            at = lane == z
            low = jnp.where(at, field[z] if z == 0 else pltpu.roll(field[z], z, 1), low)
            high = jnp.where(at, pltpu.roll(field[z], z + 1, 1), high)
        hsend_ref[r, 0] = low
        hsend_ref[r, 1] = high
        hsend_ref[r, 2] = jnp.concatenate([m[0:1, :] for m in field], axis=0)
        hsend_ref[r, 3] = jnp.concatenate([m[7:8, :] for m in field], axis=0)

    def start_halo(r):
        for side in range(4):
            halo_copy(r, side).start()

    def take_halo(r):
        for side in range(4):
            halo_copy(r, side).wait_recv()
        return [hrecv_ref[r, side] for side in range(4)]

    def neighbours(field, halo, z):
        m = field[z]
        after, before, above, below = halo
        y_up = jnp.where(lane == 127, pltpu.roll(after, 127 - z, 1), pltpu.roll(m, 127, 1))
        shifted = before if z == 0 else pltpu.roll(before, 128 - z, 1)
        y_down = jnp.where(lane == 0, shifted, pltpu.roll(m, 1, 1))
        x_up = jnp.where(sub == 7, above[z : z + 1, :], pltpu.roll(m, 7, 0))
        x_down = jnp.where(sub == 0, below[z : z + 1, :], pltpu.roll(m, 1, 0))
        return x_up, x_down, y_up, y_down

    def start_all(r):
        def one(k, carry):
            t = lax.rem(me + k, tiles)
            pltpu.make_async_remote_copy(
                src_ref=send_ref.at[r, t],
                dst_ref=recv_ref.at[r, me],
                send_sem=send_sem.at[r],
                recv_sem=recv_sem.at[r],
                device_id=place(t),
                device_id_type=MESH,
            ).start()
            return carry

        lax.fori_loop(1, tiles, one, 0)

    def wait_rows(ref, sem, r):
        part = ref.at[r, pl.ds(0, tiles - 1)]
        pltpu.make_async_copy(part, part, sem.at[r]).wait()

    def take_all(r):
        wait_rows(recv_ref, recv_sem, r)
        return jnp.where(row_t == me, send_ref[r][:, 0, :], recv_ref[r][:, 0, :])

    def put_all(r, message):
        send_ref[r] = message.reshape(tiles, 1, 128)

    def put_cross(r, field, weights):
        table = jnp.concatenate(field, axis=0)
        found = pick(table, cols_ref[...], rows_ref[...])
        first = jnp.concatenate([found[:, j * 128 : (j + 1) * 128] for j in range(half)], axis=0)
        values = jnp.concatenate([first, pltpu.roll(first, SLOT, 1)], axis=0)
        outgoing = spread(flat(weights), owner_ref[...], ranko_ref[...])
        put_all(r, jnp.where(lane_t < SLOT, values, outgoing))

    def take_cross(r):
        message = take_all(r)
        incoming = jnp.where(left_half, pltpu.roll(message[:half], SLOT, 1), message[half:])
        cells = spread(packed_lanes(incoming), rows_ref[...], cols_ref[0:128, :])
        seg_values = folded(pick(message, rankv_ref[...], owner_ref[...]))
        return [cells[8 * z : 8 * z + 8] for z in range(layers)], seg_values

    owner = flat(tile_ref[...])
    cell = flat(cell_ref[...])
    cell_row = (flat(layer_ref[...]) * width_x + cell // width_y).astype(f32)
    cell_col = (cell % width_y).astype(f32)
    owner_hot = hot(iota((tiles, segments), 0) == owner)
    owner_ref[...] = owner_hot
    groups = segments // 128
    stacked = jnp.concatenate(
        [owner_hot[:, g * 128 : (g + 1) * 128] for g in range(groups)], axis=0
    ).astype(bf16)
    tri_row = iota((128, 256), 0)
    tri_col = iota((128, 256), 1)
    counted = dot_nn(stacked, hot((tri_row < tri_col) | (tri_col >= 128)).astype(bf16))
    base = jnp.zeros((tiles, 128), f32)
    ranks = []
    for g in range(groups):
        part = counted[g * tiles : (g + 1) * tiles]
        here = owner_hot[:, g * 128 : (g + 1) * 128] * (part[:, :128] + base)
        ranks.append(jnp.sum(here, axis=0, keepdims=True))
        base = base + part[:, 128:]
    rank = jnp.concatenate(ranks, axis=1).astype(jnp.int32)
    slot = iota((128, segments), 0)
    rank_low = slot == rank
    rank_high = slot == rank + SLOT
    low_hot = hot(rank_low).astype(bf16)
    rankv_ref[0:128, :] = low_hot
    rankv_ref[128:256, :] = low_hot
    ranko_ref[...] = hot(rank_high).astype(bf16)
    asked = jnp.where(rank_low, cell_row + 1.0, jnp.where(rank_high, cell_col + 1.0, 0.0))
    put_all(0, dot_nt(owner_hot.astype(bf16), asked.astype(bf16)))

    def each_block(ref, c):
        return ref[...][:, c : c + 1]

    fsub = iota((8, block_len), 0)
    flane = iota((8, block_len), 1)
    info = jnp.zeros((8, 128), f32)
    from_hot = jnp.zeros((8, block_len), f32)
    joined_hot = []
    for c in range(blocks):
        delta, to = each_block(delta_ref, c), each_block(to_ref, c)
        info = jnp.where(
            sub == c, jnp.where(lane < 64, delta.astype(f32), to.astype(f32)), info
        )
        joined_hot.append(hot((fsub == c + delta) & (flane == to)))
        from_hot = jnp.where(
            (fsub == c) & (flane == each_block(from_ref, c)), each_block(itrans_ref, c), from_hot
        )
    cond = [cond_ref[z] for z in range(layers)]
    put_halo(0, cond, info)

    pl.semaphore_wait(barrier, tiles - 1)
    start_all(0)
    start_halo(0)
    following = pltpu.make_async_remote_copy(
        src_ref=pfrac_ref,
        dst_ref=next_ref,
        send_sem=next_sem.at[0],
        recv_sem=next_sem.at[1],
        device_id=halo_to[0],
        device_id_type=MESH,
    )
    following.start()

    position = flane
    coupling_mf, coupling_fm = padded(mf_ref), padded(fm_ref)
    press_f = padded(pfrac_ref)
    t_next = jnp.where(position < block_len - 1, padded(chain_ref), 0.0)
    t_prev = jnp.where(position > 0, pltpu.roll(t_next, 1, 1), 0.0)
    diag_f = padded(afrac_ref) + t_next + t_prev + coupling_fm
    diag_f = jnp.where(fsub < blocks, diag_f, 1.0)

    def chain(field, after, before):
        return after * pltpu.roll(field, block_len - 1, 1) + before * pltpu.roll(field, 1, 1)

    frac_ref[0] = t_next
    frac_ref[1] = t_prev
    frac_ref[2] = coupling_mf
    frac_ref[3] = coupling_fm
    frac_ref[4] = 1.0 / diag_f
    frac_ref[5] = from_hot

    well_cell = wcell_ref[...]
    wells = well_cell.shape[1]
    rate = jnp.where(wtile_ref[...] == me, wrate_ref[...], 0.0)
    well_rows = hot(iota((width_x, wells), 0) == well_cell // width_y) * rate
    well_cols = hot(iota((width_y, wells), 0) == well_cell % width_y)
    source = lax.dot_general(
        well_rows,
        well_cols,
        (((1,), (1,)), ((), ())),
        precision=lax.Precision.HIGHEST,
        preferred_element_type=f32,
    )

    asked_here = take_all(0)
    first, second = asked_here[:half], asked_here[half:]
    want_row = packed_lanes(jnp.where(left_half, first, pltpu.roll(second, SLOT, 1)))
    want_col = packed_lanes(jnp.where(left_half, pltpu.roll(first, SLOT, 1), second))
    slots = tiles * SLOT
    rows_ref[...] = hot(
        iota((layers * width_x, slots), 0) + 1 == want_row.astype(jnp.int32)
    )
    want_hot = hot(iota((width_y, slots), 0) + 1 == want_col.astype(jnp.int32)).astype(bf16)
    cols_ref[0:128, :] = want_hot
    cols_ref[128:256, :] = want_hot

    press = [press_ref[z] for z in range(layers)]
    put_halo(1, press, jnp.zeros((8, 128), f32))
    put_cross(1, press, coupling_mf * press_f)
    start_all(1)
    start_halo(1)

    halo = take_halo(0)
    along_y = gy * n_af + af
    inside_y_up = (lane < 127) | (along_y < n_gy * n_af - 1)
    inside_y_down = (lane > 0) | (along_y > 0)
    inside_x_up = (sub < 7) | (gx < n_gx - 1)
    inside_x_down = (sub > 0) | (gx > 0)
    inside = (inside_x_up, inside_x_down, inside_y_up, inside_y_down)
    diag = []
    for z in range(layers):
        total = accum_ref[z]
        near = neighbours(cond, halo, z)
        for i in range(4):
            face = jnp.where(inside[i], harmonic(cond[z], near[i]), 0.0)
            trans_ref[i, z] = face
            total = total + face
        if z + 1 < layers:
            trans_ref[4, z] = 0.5 * harmonic(cond[z], cond[z + 1])
            total = total + trans_ref[4, z]
        if z > 0:
            total = total + trans_ref[4, z - 1]
        invm_ref[z] = 1.0 / total
        diag.append(total)

    for c in range(blocks):
        inter_ref[c] = jnp.where(fsub < blocks, joined_hot[c], 0.0)
        delta = halo[1][c : c + 1, 32:33].astype(jnp.int32)
        to = halo[1][c : c + 1, 64:65].astype(jnp.int32)
        inter_ref[blocks + c] = hot(
            (fsub < blocks) & (fsub + blocks == c + delta) & (flane == to)
        )

    following.wait_recv()
    joined = jnp.concatenate([pfrac_ref[...], next_ref[...]], axis=0)
    crossing = jnp.zeros((8, block_len), f32)
    for c in range(blocks):
        found = jnp.sum(joined_hot[c] * joined, axis=1, keepdims=True)
        found = jnp.sum(found, axis=0, keepdims=True)
        crossing = jnp.where(fsub == c, from_hot * found, crossing)

    def stencil(field, halo, z):
        near = neighbours(field, halo, z)
        total = trans_ref[0, z] * near[0]
        for i in range(1, 4):
            total = total + trans_ref[i, z] * near[i]
        if z + 1 < layers:
            total = total + trans_ref[4, z] * field[z + 1]
        if z > 0:
            total = total + trans_ref[4, z - 1] * field[z - 1]
        return total

    halo = take_halo(1)
    around = [stencil(press, halo, z) for z in range(layers)]
    cells, seg_values = take_cross(1)
    for z in range(layers):
        res = diag[z] * press[z] - around[z] - cells[z] - source
        resm_ref[z] = res
        adjm_ref[z] = res * invm_ref[z]
    res_f = diag_f * press_f - chain(press_f, t_next, t_prev) - coupling_fm * seg_values - crossing
    resf_ref[...] = res_f[:blocks]
    adjf_ref[...] = (res_f * frac_ref[4])[:blocks]

    def sweep(r, carry):
        field = [adjm_ref[z] for z in range(layers)]
        frac = padded(adjf_ref)
        sent = jnp.sum(frac_ref[5] * frac, axis=1, keepdims=True)
        put_halo(r, field, jnp.broadcast_to(sent, (8, 128)))
        start_halo(r)
        put_cross(r, field, frac_ref[3] * frac)
        start_all(r)
        total = padded(resf_ref) + chain(frac, frac_ref[0], frac_ref[1])
        for c in range(blocks):
            total = total + inter_ref[c] * sent[c : c + 1, :]
        halo = take_halo(r)
        around = [stencil(field, halo, z) for z in range(layers)]
        for c in range(blocks):
            total = total + inter_ref[blocks + c] * halo[1][c : c + 1, 64:65]
        cells, seg_values = take_cross(r)
        for z in range(layers):
            adjm_ref[z] = (resm_ref[z] + around[z] + cells[z]) * invm_ref[z]
        total = total + frac_ref[2] * seg_values
        adjf_ref[...] = (total * frac_ref[4])[:blocks]
        return carry

    lax.fori_loop(2, ROUNDS, sweep, 0)

    following.wait_send()

    def finish(r, carry):
        wait_rows(send_ref, send_sem, r)
        for side in range(4):
            halo_copy(r, side).wait_send()
        return carry

    lax.fori_loop(0, ROUNDS, finish, 0)


def body(sizes, *args):
    press_matrix, press_frac = args[0], args[3]
    args = list(args)
    for i in range(11, 18):
        args[i] = args[i].reshape(1, -1)
    tiles = sizes[0] * sizes[1] * sizes[2]
    layers, width_x, width_y = press_matrix.shape
    blocks, block_len = press_frac.shape
    segments = blocks * block_len
    slots = tiles * SLOT
    vmem = pl.BlockSpec(memory_space=pltpu.VMEM)
    matrix = jax.ShapeDtypeStruct(press_matrix.shape, f32)
    fracture = jax.ShapeDtypeStruct(press_frac.shape, f32)
    return pl.pallas_call(
        functools.partial(kernel, sizes),
        out_shape=(matrix, fracture, matrix, fracture),
        in_specs=[vmem] * 18,
        out_specs=(vmem,) * 4,
        scratch_shapes=[
            pltpu.VMEM((5, layers, width_x, width_y), f32),
            pltpu.VMEM((layers, width_x, width_y), f32),
            pltpu.VMEM((6, 8, block_len), f32),
            pltpu.VMEM((2 * blocks, 8, block_len), f32),
            pltpu.VMEM((2 * width_y, slots), bf16),
            pltpu.VMEM((layers * width_x, slots), f32),
            pltpu.VMEM((tiles, segments), f32),
            pltpu.VMEM((256, segments), bf16),
            pltpu.VMEM((128, segments), bf16),
            pltpu.VMEM((ROUNDS, tiles, 1, 128), f32),
            pltpu.VMEM((ROUNDS, tiles, 1, 128), f32),
            pltpu.VMEM((ROUNDS, 4, 8, 128), f32),
            pltpu.VMEM((ROUNDS, 4, 8, 128), f32),
            pltpu.VMEM((blocks, block_len), f32),
            pltpu.SemaphoreType.DMA((ROUNDS,)),
            pltpu.SemaphoreType.DMA((ROUNDS,)),
            pltpu.SemaphoreType.DMA((ROUNDS, 4)),
            pltpu.SemaphoreType.DMA((ROUNDS, 4)),
            pltpu.SemaphoreType.DMA((2,)),
        ],
        compiler_params=pltpu.CompilerParams(
            collective_id=0, has_side_effects=True, vmem_limit_bytes=40 * 1024 * 1024
        ),
    )(*args)


def solution(mesh):
    slab = P(None, "gx", ("gy", "af"))
    fracture = P(("gx", "gy", "af"), None)
    block = P(("gx", "gy", "af"))
    in_specs = (slab,) * 3 + (fracture,) * 8 + (block,) * 4 + (P(),) * 3
    out_specs = (slab, fracture, slab, fracture)
    sizes = tuple(mesh.shape[axis] for axis in ("gx", "gy", "af"))
    return jax.shard_map(
        functools.partial(body, sizes),
        mesh=mesh,
        in_specs=in_specs,
        out_specs=out_specs,
        check_vma=False,
    )
```

time: 397 us -> 70.8 us (0.18)
  starting transfers between devices: 147 us -> 0 us
  waiting for transfers between devices: 112 us -> 0 us
  local copies, waits for them, and re-layouts: 77.7 us -> 12.1 us
  Pallas kernels: 0 us -> 57.5 us
  matrix products: 34.5 us -> 0 us
  other arithmetic: 20.3 us -> 0 us
    all_to_all x17 -> x0, waiting for transfers between devices: 88.2 us -> none  [the longest x8 51.6 us: cross(): lax.all_to_all(values, ('gx', 'gy', 'af'), split_axis=0, concat_axis=0, t...]
    ppermute x40 -> x0, starting transfers between devices: 75.2 us -> none  [the longest x16 39 us: padded_2(): lax.ppermute(tail, axis, [(i, (i + 1) % count) for i in range(ends)])]
    all_to_all x17 -> x0, starting transfers between devices: 72.2 us -> none  [the longest x8 42.6 us: cross(): lax.all_to_all(values, ('gx', 'gy', 'af'), split_axis=0, concat_axis=0, t...]
    pallas_call x0 -> x1, Pallas kernels: none -> 57.5 us  [body(): pl.pallas_call(functools.partial(kernel, sizes), out_shape=(matrix, fract...]
    gather x13 -> x0, local copies, waits for them, and re-layouts: 55 us -> none  [the longest x11 49.8 us: body(): first_seen = jnp.searchsorted(sorted_owner, sorted_owner, side='left')]
    dot_general x32 -> x0, matrix products: 34.5 us -> none  [the longest x8 10.4 us: cross(): lax.dot_general(row_hot, spread, (((0,), (0,)), ((), ())), precision=high...]
    ppermute x40 -> x0, waiting for transfers between devices: 24.1 us -> none  [the longest x16 22.8 us: padded_2(): lax.ppermute(head, axis, [((i + 1) % count, i) for i in range(ends)])]
    scatter x2 -> x0, local copies, waits for them, and re-layouts: 8.63 us -> none  [the longest x1 4.31 us: body(): requests = jnp.zeros((tiles * capacity,), jnp.int32).at[slot_index].set(l...]
  transfers between devices with their start and end apart: 57 -> 0, of which waited for: 24 -> 0; matrix products, arithmetic and copies ran while one was open for 10% -> 0% of each run, Pallas kernels for 0% -> 0%
where the time goes in v1:
time: 70.8 us; the launch traced here: 70.3 us
  Pallas kernels  57.5 us (81%)
  local copies, waits for them, and re-layouts  12.1 us (17%)
    pallas_call x1, Pallas kernels, body(): pl.pallas_call(functools.partial(kernel, sizes), out_shape=(matrix, fract...  57.5 us
    unnamed x40, local copies, waits for them, and re-layouts  12.1 us

profile of v1, /device:TPU:0, one launch (start us, length us, event | category | flops | bytes accessed | tf_op | source)
XLA Modules:
  0.0 70.3 jit_solution(5861434844805212153)
XLA Ops:
  0.6 0.0 copy-start.5
  0.6 0.0 copy-start.4
  0.7 0.6 copy-done.5
  1.3 0.0 copy-done.4
  1.3 0.0 copy-done.3
  1.4 0.0 copy-done.11
  1.4 0.8 %copy-done = f32[8,8,128]{2,1,0:T(8,128)S(1)} copy-done((f32[8,8,128]{2,1,0:T(8,128)S(1)}, f32[8,8,128]{2,1,0:T(8,128)}, u32[]{:S(2)}) %copy-start) | copy-done | bytes 32792
  2.1 0.8 %copy-done.1 = f32[8,8,128]{2,1,0:T(8,128)S(1)} copy-done((f32[8,8,128]{2,1,0:T(8,128)S(1)}, f32[8,8,128]{2,1,0:T(8,128)}, u32[]{:S(2)}) %copy-start.1) | copy-done | bytes 32792
  2.9 0.8 %copy-done.2 = f32[8,8,128]{2,1,0:T(8,128)S(1)} copy-done((f32[8,8,128]{2,1,0:T(8,128)S(1)}, f32[8,8,128]{2,1,0:T(8,128)}, u32[]{:S(2)}) %copy-start.2) | copy-done | bytes 32792
  3.6 0.7 copy-done.6
  4.3 0.7 copy-done.7
  5.0 0.7 copy-done.8
  5.7 0.7 copy-done.9
  6.4 0.7 copy-done.10
  7.1 0.7 copy-done.13
  7.7 0.7 copy-done.14
  8.4 0.7 copy-done.15
  9.0 0.7 copy-done.16
  9.7 0.7 copy-done.17
  10.4 57.5 %shard_map.201 = (f32[8,8,128]{2,1,0:T(8,128)S(1)}, f32[4,256]{1,0:T(4,128)S(1)}, f32[8,8,128]{2,1,0:T(8,128)S(1)}, f32[4,256]{1,0:T(4,128)S(1)}) custom-call(f32[8,8,128]{2,1,0:T(8,128)S(1)} %copy-done, f32[8,8,128]{2,1,0:T(8,128)S(1)} %copy-done.1, f32[8,8,128]{2,1,0:T(8,128)S(1)} %copy-done.2, f32[4,256]{1,0:T(4,128)S(1)} %copy-done.3, ...), custom_call_target="tpu_custom_call" | custom-call | tf_op jit(solution)/shard_map/pallas_call | solution.py:452
  67.9 0.6 copy.26
  68.5 0.6 copy.27
  69.1 0.6 copy.28
  69.7 0.6 copy.29
  (17 shorter events, 0.0 us)
Async XLA Ops:
  0.6 0.7 copy-start.5
  0.6 0.7 copy-start.4
  0.7 0.7 copy-start.3
  0.7 0.7 copy-start.11
  0.7 0.7 copy-start.12
  1.4 0.8 %copy-start = (f32[8,8,128]{2,1,0:T(8,128)S(1)}, f32[8,8,128]{2,1,0:T(8,128)}, u32[]{:S(2)}) copy-start(f32[8,8,128]{2,1,0:T(8,128)} %press_ref.1) | copy-start | bytes 98308
  2.1 0.8 %copy-start.1 = (f32[8,8,128]{2,1,0:T(8,128)S(1)}, f32[8,8,128]{2,1,0:T(8,128)}, u32[]{:S(2)}) copy-start(f32[8,8,128]{2,1,0:T(8,128)} %cond_ref.1) | copy-start | bytes 98308
  2.9 0.8 %copy-start.2 = (f32[8,8,128]{2,1,0:T(8,128)S(1)}, f32[8,8,128]{2,1,0:T(8,128)}, u32[]{:S(2)}) copy-start(f32[8,8,128]{2,1,0:T(8,128)} %accum_ref.1) | copy-start | bytes 98308
  3.6 0.7 copy-start.6
  4.3 0.7 copy-start.7
  5.0 0.7 copy-start.8
  5.7 0.7 copy-start.9
  6.4 0.7 copy-start.10
  7.1 0.7 copy-start.13
  7.7 0.7 copy-start.14
  8.4 0.7 copy-start.15
  9.0 0.7 copy-start.16
  9.7 0.7 copy-start.17

commit v2 on v1

v2 whole, which is shorter than its diff:
```python
import functools

import jax
import jax.numpy as jnp
from jax import lax
from jax.experimental import pallas as pl
from jax.experimental.pallas import tpu as pltpu
from jax.sharding import PartitionSpec as P

ITERS = 8
ROUNDS = ITERS + 1
SLOT = 64
LOGICAL = pl.DeviceIdType.LOGICAL
f32 = jnp.float32
bf16 = jnp.bfloat16


def harmonic(first, second):
    return 2.0 * first * second / (first + second)


def iota(shape, dim):
    return lax.broadcasted_iota(jnp.int32, shape, dim)


def hot(mask):
    return jnp.where(mask, 1.0, 0.0)


def pieces(values):
    high = values.astype(bf16)
    return high, (values - high.astype(f32)).astype(bf16)


def dot_nn(a, b):
    return lax.dot_general(a, b, (((1,), (0,)), ((), ())), preferred_element_type=f32)


def dot_nt(a, b):
    return lax.dot_general(a, b, (((1,), (1,)), ((), ())), preferred_element_type=f32)


def taken(row, lanes):
    return jnp.take_along_axis(
        jnp.broadcast_to(row, lanes.shape), lanes, axis=1, mode="promise_in_bounds"
    )


def by_eight(x):
    return [x[8 * q : 8 * q + 8] for q in range(x.shape[0] // 8)]


def kernel(sizes, *refs):
    hbm, outs, held, rest = refs[:18], refs[18:22], refs[22:40], refs[40:]
    resm_ref, resf_ref, adjm_ref, adjf_ref = outs
    (
        trans_ref,
        invm_ref,
        frac_ref,
        inter_ref,
        cols_ref,
        rows_ref,
        index_ref,
        slot_ref,
        seg_ref,
        send_ref,
        recv_ref,
        hsend_ref,
        hrecv_ref,
        next_ref,
        load_sem,
        send_sem,
        recv_sem,
        hsend_sem,
        hrecv_sem,
        next_sem,
    ) = rest
    n_gx, n_gy, n_af = sizes
    tiles = n_gx * n_gy * n_af
    half = tiles // 2
    gx, gy, af = lax.axis_index("gx"), lax.axis_index("gy"), lax.axis_index("af")
    me = (gx * n_gy + gy) * n_af + af
    barrier = pltpu.get_barrier_semaphore()

    loads = [pltpu.make_async_copy(hbm[i], held[i], load_sem.at[i]) for i in range(18)]
    for i in (8, 9, 10, 1, 11, 13, 3, 12, 14, 0, 4, 5, 6, 7, 15, 16, 17, 2):
        loads[i].start()

    def wrapped(k):
        return lax.rem(me + k, tiles)

    for k in range(1, tiles):
        pl.semaphore_signal(
            barrier, inc=1, device_id=wrapped(k), device_id_type=LOGICAL
        )

    def loaded(i):
        loads[i].wait()
        return held[i]

    press_ref, cond_ref = held[0], held[1]
    layers, width_x, width_y = press_ref.shape
    blocks, block_len = held[3].shape

    lane = iota((8, 128), 1)
    sub = iota((8, 128), 0)
    block_of = sub % blocks
    position = lane + 128 * (sub // blocks)
    row_t = iota((tiles, 128), 0)
    lane_t = iota((tiles, 128), 1)
    left_half = iota((half, 128), 1) < SLOT

    def folded(x):
        return jnp.concatenate([x[:, :128], x[:, 128:]], axis=0)

    def unfolded(x):
        return jnp.concatenate([x[:blocks], x[blocks:]], axis=1)

    halo_to = (
        wrapped(tiles - 1),
        wrapped(1),
        wrapped(tiles - n_gy * n_af),
        wrapped(n_gy * n_af),
    )

    def halo_copy(r, side):
        return pltpu.make_async_remote_copy(
            src_ref=hsend_ref.at[r, side],
            dst_ref=hrecv_ref.at[r, side],
            send_sem=hsend_sem.at[r, side],
            recv_sem=hrecv_sem.at[r, side],
            device_id=halo_to[side],
            device_id_type=LOGICAL,
        )

    def put_halo(r, field, extra):
        low = jnp.zeros((8, 128), f32)
        high = extra
        for z in range(layers):
            at = lane == z
            low = jnp.where(at, field[z] if z == 0 else pltpu.roll(field[z], z, 1), low)
            high = jnp.where(at, pltpu.roll(field[z], z + 1, 1), high)
        hsend_ref[r, 0] = low
        hsend_ref[r, 1] = high
        hsend_ref[r, 2] = jnp.concatenate([m[0:1, :] for m in field], axis=0)
        hsend_ref[r, 3] = jnp.concatenate([m[7:8, :] for m in field], axis=0)

    def start_halo(r):
        for side in range(4):
            halo_copy(r, side).start()

    def take_halo(r):
        for side in range(4):
            halo_copy(r, side).wait_recv()
        return [hrecv_ref[r, side] for side in range(4)]

    def neighbours(field, halo, z):
        m = field[z]
        after, before, above, below = halo
        y_up = jnp.where(lane == 127, pltpu.roll(after, 127 - z, 1), pltpu.roll(m, 127, 1))
        shifted = before if z == 0 else pltpu.roll(before, 128 - z, 1)
        y_down = jnp.where(lane == 0, shifted, pltpu.roll(m, 1, 1))
        x_up = jnp.where(sub == 7, above[z : z + 1, :], pltpu.roll(m, 7, 0))
        x_down = jnp.where(sub == 0, below[z : z + 1, :], pltpu.roll(m, 1, 0))
        return x_up, x_down, y_up, y_down

    def start_all(r):
        for k in range(1, tiles):
            t = wrapped(k)
            pltpu.make_async_remote_copy(
                src_ref=send_ref.at[r, t],
                dst_ref=recv_ref.at[r, me],
                send_sem=send_sem.at[r],
                recv_sem=recv_sem.at[r],
                device_id=t,
                device_id_type=LOGICAL,
            ).start()

    def wait_rows(ref, sem, r):
        part = ref.at[r, pl.ds(0, tiles - 1)]
        pltpu.make_async_copy(part, part, sem.at[r]).wait()

    def put_all(r, message):
        send_ref[r] = message.reshape(tiles, 1, 128)
        recv_ref[r, me] = send_ref[r, me]

    def take_all(r):
        wait_rows(recv_ref, recv_sem, r)
        return recv_ref[r][:, 0, :]

    def put_cross(r, field_ref, weights):
        wanted = []
        for q in range(half // 8):
            at_row = index_ref[0, 8 * q : 8 * q + 8]
            at_lane = index_ref[1, 8 * q : 8 * q + 8]
            found = jnp.zeros((8, 128), f32)
            for z in range(layers):
                for x in range(width_x):
                    got = taken(field_ref[z, x : x + 1, :], at_lane)
                    found = jnp.where(at_row == z * width_x + x, got, found)
            wanted.append(found)
        values = wanted + [pltpu.roll(v, SLOT, 1) for v in wanted]
        rows = [jnp.broadcast_to(weights[i : i + 1, :], (8, 128)) for i in range(8)]
        message = []
        for q in range(tiles // 8):
            at_row = slot_ref[0, 8 * q : 8 * q + 8]
            at_lane = slot_ref[1, 8 * q : 8 * q + 8]
            found = jnp.zeros((8, 128), f32)
            for i in range(8):
                found = jnp.where(at_row == i, taken(rows[i], at_lane), found)
            message.append(jnp.where(lane < SLOT, values[q], found))
        put_all(r, jnp.concatenate(message, axis=0))

    def take_cross(r):
        message = take_all(r)
        incoming = jnp.where(left_half, pltpu.roll(message[:half], SLOT, 1), message[half:])
        high, low = pieces(incoming)
        parts = []
        for piece in (high.astype(f32), low.astype(f32)):
            scaled = []
            for j in range(half):
                one = jnp.broadcast_to(piece[j : j + 1, :], (16, 128)).astype(bf16)
                wide = jnp.concatenate([one] * (layers * width_x // 16), axis=0)
                scaled.append(rows_ref[:, 128 * j : 128 * j + 128] * wide)
            parts.append(jnp.concatenate(scaled, axis=1))
        both = dot_nt(jnp.concatenate(parts, axis=0), cols_ref[...])
        cells = both[: layers * width_x] + both[layers * width_x :]
        of, rank = seg_ref[0], seg_ref[1]
        seg_values = jnp.zeros((8, 128), f32)
        for t in range(tiles):
            seg_values = jnp.where(of == t, taken(recv_ref[r, t], rank), seg_values)
        return [cells[8 * z : 8 * z + 8] for z in range(layers)], seg_values

    owner = folded(loaded(8)[...])
    layer = folded(loaded(9)[...])
    cell = folded(loaded(10)[...])
    cell_row = (layer * width_x + cell // width_y).astype(f32) + 1.0
    cell_col = (cell % width_y).astype(f32) + 1.0
    owner_hot = [hot(row_t == owner[g : g + 1, :]) for g in range(8)]
    tri_row = iota((128, 256), 0)
    tri_col = iota((128, 256), 1)
    counted = dot_nn(
        jnp.concatenate(owner_hot, axis=0).astype(bf16),
        hot((tri_row < tri_col) | (tri_col >= 128)).astype(bf16),
    )
    base = jnp.zeros((tiles, 128), f32)
    ranks = []
    for g in range(8):
        part = counted[g * tiles : (g + 1) * tiles]
        ranks.append(jnp.sum(owner_hot[g] * (part[:, :128] + base), axis=0, keepdims=True))
        base = base + part[:, 128:]
    rank = jnp.concatenate(ranks, axis=0).astype(jnp.int32)
    seg_ref[0] = owner
    seg_ref[1] = rank
    slot = iota((128, 128), 0)
    lane_up = iota((128, 128), 1).astype(f32) + 1.0
    asked, origin = [], []
    for g in range(8):
        low = slot == rank[g : g + 1, :]
        high = slot == rank[g : g + 1, :] + SLOT
        asked.append(
            jnp.where(low, cell_row[g : g + 1, :], jnp.where(high, cell_col[g : g + 1, :], 0.0))
        )
        origin.append(jnp.where(low, lane_up, jnp.where(high, g + 1.0, 0.0)))
    table = jnp.concatenate(
        [jnp.concatenate(asked, axis=1), jnp.concatenate(origin, axis=1)], axis=0
    )
    spread = dot_nt(jnp.concatenate(owner_hot, axis=1).astype(bf16), table.astype(bf16))
    put_all(0, spread[:, :128])
    origin = spread[:, 128:]
    origin_row = jnp.where(lane_t < SLOT, 0.0, origin)
    slot_ref[0] = origin_row.astype(jnp.int32) - 1
    slot_ref[1] = jnp.maximum(pltpu.roll(origin, SLOT, 1).astype(jnp.int32) - 1, 0)

    cond_ref = loaded(1)
    cond = [cond_ref[z] for z in range(layers)]
    all_delta, all_to = loaded(11)[...], loaded(13)[...]
    info = jnp.zeros((8, 128), f32)
    near_hot, next_hot = [], []
    for c in range(blocks):
        delta, to = all_delta[:, c : c + 1], all_to[:, c : c + 1]
        info = jnp.where(
            sub == c, jnp.where(lane < 64, delta.astype(f32), to.astype(f32)), info
        )
        near_hot.append(hot((block_of == c + delta) & (position == to)))
        next_hot.append(hot((block_of + blocks == c + delta) & (position == to)))
        inter_ref[c] = near_hot[c]
    put_halo(0, cond, info)
    pfrac_ref = loaded(3)

    pl.semaphore_wait(barrier, tiles - 1)
    start_all(0)
    start_halo(0)
    following = pltpu.make_async_remote_copy(
        src_ref=pfrac_ref,
        dst_ref=next_ref,
        send_sem=next_sem.at[0],
        recv_sem=next_sem.at[1],
        device_id=halo_to[0],
        device_id_type=LOGICAL,
    )
    following.start()

    all_from, all_trans = loaded(12)[...], loaded(14)[...]
    from_hot = jnp.zeros((8, 128), f32)
    for c in range(blocks):
        from_hot = jnp.where(
            (block_of == c) & (position == all_from[:, c : c + 1]),
            all_trans[:, c : c + 1],
            from_hot,
        )

    def later(x):
        moved = pltpu.roll(x, 127, 1)
        return jnp.where(lane == 127, pltpu.roll(moved, blocks, 0), moved)

    def earlier(x):
        moved = pltpu.roll(x, 1, 1)
        return jnp.where(lane == 0, pltpu.roll(moved, blocks, 0), moved)

    def chain(field, after, before):
        return after * later(field) + before * earlier(field)

    loaded(0)
    press = [press_ref[z] for z in range(layers)]
    press_f = folded(pfrac_ref[...])
    accum_f = folded(loaded(4)[...])
    t_next = jnp.where(position < block_len - 1, folded(loaded(5)[...]), 0.0)
    t_prev = jnp.where(position > 0, earlier(t_next), 0.0)
    coupling_mf = folded(loaded(6)[...])
    coupling_fm = folded(loaded(7)[...])
    diag_f = accum_f + t_next + t_prev + coupling_fm
    frac_ref[0] = t_next
    frac_ref[1] = t_prev
    frac_ref[2] = coupling_mf
    frac_ref[3] = coupling_fm
    frac_ref[4] = 1.0 / diag_f
    frac_ref[5] = from_hot

    well_tile, well_cell, well_rate = loaded(15)[...], loaded(16)[...], loaded(17)[...]
    wells = well_cell.shape[1]
    rate = jnp.where(well_tile == me, well_rate, 0.0)
    source = lax.dot_general(
        hot(iota((width_x, wells), 0) == well_cell // width_y) * rate,
        hot(iota((width_y, wells), 0) == well_cell % width_y),
        (((1,), (1,)), ((), ())),
        precision=lax.Precision.HIGHEST,
        preferred_element_type=f32,
    )
    accum_ref = loaded(2)
    put_halo(1, press, jnp.zeros((8, 128), f32))
    start_halo(1)

    halo = take_halo(0)
    along_y = gy * n_af + af
    inside = (
        (sub < 7) | (gx < n_gx - 1),
        (sub > 0) | (gx > 0),
        (lane < 127) | (along_y < n_gy * n_af - 1),
        (lane > 0) | (along_y > 0),
    )
    diag = []
    for z in range(layers):
        total = accum_ref[z]
        near = neighbours(cond, halo, z)
        for i in range(4):
            face = jnp.where(inside[i], harmonic(cond[z], near[i]), 0.0)
            trans_ref[i, z] = face
            total = total + face
        if z + 1 < layers:
            trans_ref[4, z] = 0.5 * harmonic(cond[z], cond[z + 1])
            total = total + trans_ref[4, z]
        if z > 0:
            total = total + trans_ref[4, z - 1]
        invm_ref[z] = 1.0 / total
        diag.append(total)
    for c in range(blocks):
        delta = halo[1][c : c + 1, 32:33].astype(jnp.int32)
        to = halo[1][c : c + 1, 64:65].astype(jnp.int32)
        inter_ref[blocks + c] = hot((block_of + blocks == c + delta) & (position == to))

    asked_here = take_all(0)
    first, second = asked_here[:half], asked_here[half:]
    want_row = jnp.where(left_half, first, pltpu.roll(second, SLOT, 1)).astype(jnp.int32) - 1
    want_col = jnp.where(left_half, pltpu.roll(first, SLOT, 1), second).astype(jnp.int32) - 1
    index_ref[0] = want_row
    index_ref[1] = jnp.maximum(want_col, 0)

    put_cross(1, press_ref, coupling_mf * press_f)
    start_all(1)
    for j in range(half):
        at = slice(128 * j, 128 * j + 128)
        rows_ref[:, at] = hot(
            iota((layers * width_x, 128), 0) == want_row[j : j + 1, :]
        ).astype(bf16)
        cols_ref[:, at] = hot(iota((width_y, 128), 0) == want_col[j : j + 1, :]).astype(bf16)

    following.wait_recv()
    next_f = folded(next_ref[...])
    crossing = jnp.zeros((8, 128), f32)
    for c in range(blocks):
        found = jnp.sum(near_hot[c] * press_f + next_hot[c] * next_f, axis=1, keepdims=True)
        found = jnp.sum(found, axis=0, keepdims=True)
        crossing = jnp.where(block_of == c, from_hot * found, crossing)

    def stencil(field, halo, z):
        near = neighbours(field, halo, z)
        total = trans_ref[0, z] * near[0]
        for i in range(1, 4):
            total = total + trans_ref[i, z] * near[i]
        if z + 1 < layers:
            total = total + trans_ref[4, z] * field[z + 1]
        if z > 0:
            total = total + trans_ref[4, z - 1] * field[z - 1]
        return total

    halo = take_halo(1)
    around = [stencil(press, halo, z) for z in range(layers)]
    cells, seg_values = take_cross(1)
    for z in range(layers):
        res = diag[z] * press[z] - around[z] - cells[z] - source
        resm_ref[z] = res
        adjm_ref[z] = res * invm_ref[z]
    res_f = diag_f * press_f - chain(press_f, t_next, t_prev) - coupling_fm * seg_values - crossing
    resf_ref[...] = unfolded(res_f)
    frac_ref[6] = res_f
    frac_ref[7] = res_f * frac_ref[4]

    def sweep(r, carry):
        field = [adjm_ref[z] for z in range(layers)]
        frac = frac_ref[7]
        sent = jnp.sum(frac_ref[5] * frac, axis=1, keepdims=True)
        sent = sent[:blocks] + sent[blocks:]
        put_halo(r, field, jnp.broadcast_to(jnp.concatenate([sent, sent], axis=0), (8, 128)))
        start_halo(r)
        put_cross(r, adjm_ref, frac_ref[3] * frac)
        start_all(r)
        total = frac_ref[6] + chain(frac, frac_ref[0], frac_ref[1])
        for c in range(blocks):
            total = total + inter_ref[c] * sent[c : c + 1, :]
        halo = take_halo(r)
        around = [resm_ref[z] + stencil(field, halo, z) for z in range(layers)]
        for c in range(blocks):
            total = total + inter_ref[blocks + c] * halo[1][c : c + 1, 64:65]
        cells, seg_values = take_cross(r)
        for z in range(layers):
            adjm_ref[z] = (around[z] + cells[z]) * invm_ref[z]
        frac_ref[7] = (total + frac_ref[2] * seg_values) * frac_ref[4]
        return carry

    lax.fori_loop(2, ROUNDS, sweep, 0)
    adjf_ref[...] = unfolded(frac_ref[7])

    following.wait_send()

    def finish(r, carry):
        wait_rows(send_ref, send_sem, r)
        for side in range(4):
            halo_copy(r, side).wait_send()
        return carry

    lax.fori_loop(0, ROUNDS, finish, 0)


def copy_out(*refs):
    sems = refs[8]
    copies = [pltpu.make_async_copy(refs[i], refs[4 + i], sems.at[i]) for i in range(4)]
    for copy in copies:
        copy.start()
    for copy in copies:
        copy.wait()


def body(sizes, *args):
    press_matrix, press_frac = args[0], args[3]
    args = list(args)
    for i in range(11, 18):
        args[i] = args[i].reshape(1, -1)
    tiles = sizes[0] * sizes[1] * sizes[2]
    layers, width_x, width_y = press_matrix.shape
    blocks, block_len = press_frac.shape
    slots = tiles * SLOT
    vmem = pl.BlockSpec(memory_space=pltpu.VMEM)
    anywhere = pl.BlockSpec(memory_space=pl.ANY)
    matrix = jax.ShapeDtypeStruct(press_matrix.shape, f32)
    fracture = jax.ShapeDtypeStruct(press_frac.shape, f32)
    out_shape = (matrix, fracture, matrix, fracture)
    results = pl.pallas_call(
        functools.partial(kernel, sizes),
        out_shape=out_shape,
        in_specs=[anywhere] * 18,
        out_specs=(vmem,) * 4,
        scratch_shapes=[pltpu.VMEM(x.shape, x.dtype) for x in args]
        + [
            pltpu.VMEM((5, layers, width_x, width_y), f32),
            pltpu.VMEM((layers, width_x, width_y), f32),
            pltpu.VMEM((8, 8, 128), f32),
            pltpu.VMEM((2 * blocks, 8, 128), f32),
            pltpu.VMEM((width_y, slots), bf16),
            pltpu.VMEM((layers * width_x, slots), bf16),
            pltpu.VMEM((2, tiles // 2, 128), jnp.int32),
            pltpu.VMEM((2, tiles, 128), jnp.int32),
            pltpu.VMEM((2, 8, 128), jnp.int32),
            pltpu.VMEM((ROUNDS, tiles, 1, 128), f32),
            pltpu.VMEM((ROUNDS, tiles, 1, 128), f32),
            pltpu.VMEM((ROUNDS, 4, 8, 128), f32),
            pltpu.VMEM((ROUNDS, 4, 8, 128), f32),
            pltpu.VMEM((blocks, block_len), f32),
            pltpu.SemaphoreType.DMA((18,)),
            pltpu.SemaphoreType.DMA((ROUNDS,)),
            pltpu.SemaphoreType.DMA((ROUNDS,)),
            pltpu.SemaphoreType.DMA((ROUNDS, 4)),
            pltpu.SemaphoreType.DMA((ROUNDS, 4)),
            pltpu.SemaphoreType.DMA((2,)),
        ],
        compiler_params=pltpu.CompilerParams(
            collective_id=0, has_side_effects=True, vmem_limit_bytes=60 * 1024 * 1024
        ),
    )(*args)
    return pl.pallas_call(
        copy_out,
        out_shape=out_shape,
        in_specs=[anywhere] * 4,
        out_specs=(anywhere,) * 4,
        scratch_shapes=[pltpu.SemaphoreType.DMA((4,))],
        compiler_params=pltpu.CompilerParams(vmem_limit_bytes=60 * 1024 * 1024),
    )(*results)


def solution(mesh):
    slab = P(None, "gx", ("gy", "af"))
    fracture = P(("gx", "gy", "af"), None)
    block = P(("gx", "gy", "af"))
    in_specs = (slab,) * 3 + (fracture,) * 8 + (block,) * 4 + (P(),) * 3
    out_specs = (slab, fracture, slab, fracture)
    sizes = tuple(mesh.shape[axis] for axis in ("gx", "gy", "af"))
    return jax.shard_map(
        functools.partial(body, sizes),
        mesh=mesh,
        in_specs=in_specs,
        out_specs=out_specs,
        check_vma=False,
    )
```

time: 70.8 us -> 58.2 us (0.82)
  local copies, waits for them, and re-layouts: 12.1 us -> 0 us
    unnamed x40 -> x0, local copies, waits for them, and re-layouts: 12.1 us -> none
    pallas_call x1 -> x2, Pallas kernels: 57.5 us -> 57.4 us  [the longest x1 54 us: body(): pl.pallas_call(functools.partial(kernel, sizes), out_shape=out_shape, in_...]
where the time goes in v2:
time: 58.2 us; the launch traced here: 58 us
  Pallas kernels  57.4 us (99%)
  between operations  0.65 us (1%)
    pallas_call x1, Pallas kernels, body(): pl.pallas_call(functools.partial(kernel, sizes), out_shape=out_shape, in_...  54 us
    pallas_call x1, Pallas kernels, body(): pl.pallas_call(copy_out, out_shape=out_shape, in_specs=[anywhere] * 4, ou...  3.37 us

profile of v2, /device:TPU:0, one launch (start us, length us, event | category | flops | bytes accessed | tf_op | source)
XLA Modules:
  0.0 58.0 jit_solution(5015810709937413551)
XLA Ops:
  0.6 54.0 %shard_map.201 = (f32[8,8,128]{2,1,0:T(8,128)}, f32[4,256]{1,0:T(4,128)}, f32[8,8,128]{2,1,0:T(8,128)}, f32[4,256]{1,0:T(4,128)}) custom-call(f32[8,8,128]{2,1,0:T(8,128)} %refs_0_.1, f32[8,8,128]{2,1,0:T(8,128)} %refs_1_.1, f32[8,8,128]{2,1,0:T(8,128)} %refs_2_.1, f32[4,256]{1,0:T(4,128)} %refs_3_.1, f32[4,256]{1,0:T(4,128)} %refs_4_.1, f32[4,256]{1,0:T(4,128)} %refs_5_.1, ...), custom_call_target="tpu_custom_call" | custom-call | tf_op jit(solution)/shard_map/pallas_call | solution.py:488
  54.7 3.4 %shard_map.202 = (f32[8,8,128]{2,1,0:T(8,128)}, f32[4,256]{1,0:T(4,128)}, f32[8,8,128]{2,1,0:T(8,128)}, f32[4,256]{1,0:T(4,128)}) custom-call(f32[8,8,128]{2,1,0:T(8,128)} %get-tuple-element.8.refs_0_, f32[4,256]{1,0:T(4,128)} %get-tuple-element.9.refs_1_, f32[8,8,128]{2,1,0:T(8,128)} %get-tuple-element.10.refs_2_, f32[4,256]{1,0:T(4,128)} %get-tuple-element.11.refs_3_), custom_call_target="tpu_custom_call" | custom-call | tf_op jit(solution)/shard_map/pallas_call | solution.py:520

commit v3 on v2

--- a/solution.py
+++ b/solution.py
@@ -164,15 +164,17 @@
         x_down = jnp.where(sub == 0, below[z : z + 1, :], pltpu.roll(m, 1, 0))
         return x_up, x_down, y_up, y_down
 
-    def start_all(r):
-        for k in range(1, tiles):
-            t = wrapped(k)
+    def put_eight(r, q, message):
+        send_ref[r, 8 * q : 8 * q + 8] = message.reshape(8, 1, 128)
+        if q == 0:
+            recv_ref[r, 0] = message[0:1, :]
+        for k in range(max(8 * q, 1), 8 * q + 8):
             pltpu.make_async_remote_copy(
-                src_ref=send_ref.at[r, t],
-                dst_ref=recv_ref.at[r, me],
+                src_ref=send_ref.at[r, k],
+                dst_ref=recv_ref.at[r, tiles - k],
                 send_sem=send_sem.at[r],
                 recv_sem=recv_sem.at[r],
-                device_id=t,
+                device_id=wrapped(k),
                 device_id_type=LOGICAL,
             ).start()
 
@@ -180,36 +182,27 @@
         part = ref.at[r, pl.ds(0, tiles - 1)]
         pltpu.make_async_copy(part, part, sem.at[r]).wait()
 
-    def put_all(r, message):
-        send_ref[r] = message.reshape(tiles, 1, 128)
-        recv_ref[r, me] = send_ref[r, me]
-
     def take_all(r):
         wait_rows(recv_ref, recv_sem, r)
         return recv_ref[r][:, 0, :]
 
     def put_cross(r, field_ref, weights):
-        wanted = []
+        rows = [jnp.broadcast_to(weights[i : i + 1, :], (8, 128)) for i in range(8)]
         for q in range(half // 8):
             at_row = index_ref[0, 8 * q : 8 * q + 8]
             at_lane = index_ref[1, 8 * q : 8 * q + 8]
-            found = jnp.zeros((8, 128), f32)
+            wanted = jnp.zeros((8, 128), f32)
             for z in range(layers):
                 for x in range(width_x):
                     got = taken(field_ref[z, x : x + 1, :], at_lane)
-                    found = jnp.where(at_row == z * width_x + x, got, found)
-            wanted.append(found)
-        values = wanted + [pltpu.roll(v, SLOT, 1) for v in wanted]
-        rows = [jnp.broadcast_to(weights[i : i + 1, :], (8, 128)) for i in range(8)]
-        message = []
-        for q in range(tiles // 8):
-            at_row = slot_ref[0, 8 * q : 8 * q + 8]
-            at_lane = slot_ref[1, 8 * q : 8 * q + 8]
-            found = jnp.zeros((8, 128), f32)
-            for i in range(8):
-                found = jnp.where(at_row == i, taken(rows[i], at_lane), found)
-            message.append(jnp.where(lane < SLOT, values[q], found))
-        put_all(r, jnp.concatenate(message, axis=0))
+                    wanted = jnp.where(at_row == z * width_x + x, got, wanted)
+            for p, values in ((q + half // 8, pltpu.roll(wanted, SLOT, 1)), (q, wanted)):
+                at_row = slot_ref[0, 8 * p : 8 * p + 8]
+                at_lane = slot_ref[1, 8 * p : 8 * p + 8]
+                found = jnp.zeros((8, 128), f32)
+                for i in range(8):
+                    found = jnp.where(at_row == i, taken(rows[i], at_lane), found)
+                put_eight(r, p, jnp.where(lane < SLOT, values, found))
 
     def take_cross(r):
         message = take_all(r)
@@ -231,7 +224,8 @@
             seg_values = jnp.where(of == t, taken(recv_ref[r, t], rank), seg_values)
         return [cells[8 * z : 8 * z + 8] for z in range(layers)], seg_values
 
-    owner = folded(loaded(8)[...])
+    owner = folded(loaded(8)[...]) - me
+    owner = jnp.where(owner < 0, owner + tiles, owner)
     layer = folded(loaded(9)[...])
     cell = folded(loaded(10)[...])
     cell_row = (layer * width_x + cell // width_y).astype(f32) + 1.0
@@ -266,7 +260,7 @@
         [jnp.concatenate(asked, axis=1), jnp.concatenate(origin, axis=1)], axis=0
     )
     spread = dot_nt(jnp.concatenate(owner_hot, axis=1).astype(bf16), table.astype(bf16))
-    put_all(0, spread[:, :128])
+    requests = spread[:, :128]
     origin = spread[:, 128:]
     origin_row = jnp.where(lane_t < SLOT, 0.0, origin)
     slot_ref[0] = origin_row.astype(jnp.int32) - 1
@@ -289,7 +283,8 @@
     pfrac_ref = loaded(3)
 
     pl.semaphore_wait(barrier, tiles - 1)
-    start_all(0)
+    for q in (*range(half // 8, tiles // 8), *range(half // 8)):
+        put_eight(0, q, requests[8 * q : 8 * q + 8])
     start_halo(0)
     following = pltpu.make_async_remote_copy(
         src_ref=pfrac_ref,
@@ -387,7 +382,6 @@
     index_ref[1] = jnp.maximum(want_col, 0)
 
     put_cross(1, press_ref, coupling_mf * press_f)
-    start_all(1)
     for j in range(half):
         at = slice(128 * j, 128 * j + 128)
         rows_ref[:, at] = hot(
@@ -431,10 +425,9 @@
         frac = frac_ref[7]
         sent = jnp.sum(frac_ref[5] * frac, axis=1, keepdims=True)
         sent = sent[:blocks] + sent[blocks:]
+        put_cross(r, adjm_ref, frac_ref[3] * frac)
         put_halo(r, field, jnp.broadcast_to(jnp.concatenate([sent, sent], axis=0), (8, 128)))
         start_halo(r)
-        put_cross(r, adjm_ref, frac_ref[3] * frac)
-        start_all(r)
         total = frac_ref[6] + chain(frac, frac_ref[0], frac_ref[1])
         for c in range(blocks):
             total = total + inter_ref[c] * sent[c : c + 1, :]
@@ -487,7 +480,7 @@
     out_shape = (matrix, fracture, matrix, fracture)
     results = pl.pallas_call(
         functools.partial(kernel, sizes),
-        out_shape=out_shape,
+        out_shape=tuple(pltpu.VMEM(x.shape, f32) for x in out_shape),
         in_specs=[anywhere] * 18,
         out_specs=(vmem,) * 4,
         scratch_shapes=[pltpu.VMEM(x.shape, x.dtype) for x in args]
@@ -520,10 +513,10 @@
     return pl.pallas_call(
         copy_out,
         out_shape=out_shape,
-        in_specs=[anywhere] * 4,
+        in_specs=[vmem] * 4,
         out_specs=(anywhere,) * 4,
         scratch_shapes=[pltpu.SemaphoreType.DMA((4,))],
-        compiler_params=pltpu.CompilerParams(vmem_limit_bytes=60 * 1024 * 1024),
+        compiler_params=pltpu.CompilerParams(vmem_limit_bytes=4 * 1024 * 1024),
     )(*results)
 
 

time: 58.2 us -> 54.7 us (0.940)
  Pallas kernels: 57.4 us -> 53.8 us
    pallas_call x2, Pallas kernels: 57.4 us -> 53.8 us  [the longest x1 53.2 us: body(): pl.pallas_call(functools.partial(kernel, sizes), out_shape=tuple((pltpu.V...]
where the time goes in v3:
time: 54.7 us; the launch traced here: 54.5 us
  Pallas kernels  53.8 us (98%)
  between operations  0.65 us (1%)
    pallas_call x1, Pallas kernels, body(): pl.pallas_call(functools.partial(kernel, sizes), out_shape=tuple((pltpu.V...  53.2 us

profile of v3, /device:TPU:0, one launch (start us, length us, event | category | flops | bytes accessed | tf_op | source)
XLA Modules:
  0.0 54.5 jit_solution(9103403659766017282)
XLA Ops:
  0.6 53.2 %shard_map.201 = (f32[8,8,128]{2,1,0:T(8,128)S(1)}, f32[4,256]{1,0:T(4,128)S(1)}, f32[8,8,128]{2,1,0:T(8,128)S(1)}, f32[4,256]{1,0:T(4,128)S(1)}) custom-call(f32[8,8,128]{2,1,0:T(8,128)} %refs_0_.1, f32[8,8,128]{2,1,0:T(8,128)} %refs_1_.1, f32[8,8,128]{2,1,0:T(8,128)} %refs_2_.1, f32[4,256]{1,0:T(4,128)} %refs_3_.1, f32[4,256]{1,0:T(4,128)} %refs_4_.1, ...), custom_call_target="tpu_custom_call" | custom-call | tf_op jit(solution)/shard_map/pallas_call | solution.py:481
  53.8 0.7 %shard_map.202 = (f32[8,8,128]{2,1,0:T(8,128)}, f32[4,256]{1,0:T(4,128)}, f32[8,8,128]{2,1,0:T(8,128)}, f32[4,256]{1,0:T(4,128)}) custom-call(f32[8,8,128]{2,1,0:T(8,128)S(1)} %get-tuple-element.8.refs_0_, f32[4,256]{1,0:T(4,128)S(1)} %get-tuple-element.9.refs_1_, f32[8,8,128]{2,1,0:T(8,128)S(1)} %get-tuple-element.10.refs_2_, ...), custom_call_target="tpu_custom_call" | custom-call | tf_op jit(solution)/shard_map/pallas_call | solution.py:513

commit v4 on v3

--- a/solution.py
+++ b/solution.py
@@ -64,12 +64,17 @@
         slot_ref,
         seg_ref,
         send_ref,
+        stage_ref,
+        mid_ref,
+        pass_ref,
         recv_ref,
         hsend_ref,
         hrecv_ref,
         next_ref,
         load_sem,
         send_sem,
+        mid_sem,
+        pass_sem,
         recv_sem,
         hsend_sem,
         hrecv_sem,
@@ -79,7 +84,9 @@
     tiles = n_gx * n_gy * n_af
     half = tiles // 2
     gx, gy, af = lax.axis_index("gx"), lax.axis_index("gy"), lax.axis_index("af")
-    me = (gx * n_gy + gy) * n_af + af
+    planes = n_gx * n_gy
+    plane = gx * n_gy + gy
+    me = plane * n_af + af
     barrier = pltpu.get_barrier_semaphore()
 
     loads = [pltpu.make_async_copy(hbm[i], held[i], load_sem.at[i]) for i in range(18)]
@@ -89,6 +96,8 @@
     def wrapped(k):
         return lax.rem(me + k, tiles)
 
+    beside = [plane * n_af + lax.rem(af + k, n_af) for k in range(n_af)]
+    across = [wrapped(k * n_af) for k in range(planes)]
     for k in range(1, tiles):
         pl.semaphore_signal(
             barrier, inc=1, device_id=wrapped(k), device_id_type=LOGICAL
@@ -164,30 +173,56 @@
         x_down = jnp.where(sub == 0, below[z : z + 1, :], pltpu.roll(m, 1, 0))
         return x_up, x_down, y_up, y_down
 
-    def put_eight(r, q, message):
-        send_ref[r, 8 * q : 8 * q + 8] = message.reshape(8, 1, 128)
-        if q == 0:
-            recv_ref[r, 0] = message[0:1, :]
-        for k in range(max(8 * q, 1), 8 * q + 8):
+    def put_rows(r, message):
+        for q in range(tiles // 8):
+            stage_ref[8 * q : 8 * q + 8] = message[q].reshape(8, 1, 128)
+        for p in range(tiles):
+            i, j = p % n_af, p // n_af
+            row = stage_ref[p]
+            if i > 0:
+                send_ref[r, i * planes + j] = row
+            elif j > 0:
+                pass_ref[r, j * n_af] = row
+            else:
+                recv_ref[r, 0] = row
+        for i in range(1, n_af):
             pltpu.make_async_remote_copy(
-                src_ref=send_ref.at[r, k],
-                dst_ref=recv_ref.at[r, tiles - k],
+                src_ref=send_ref.at[r, pl.ds(i * planes, planes)],
+                dst_ref=mid_ref.at[r, pl.ds((n_af - i) * planes, planes)],
                 send_sem=send_sem.at[r],
-                recv_sem=recv_sem.at[r],
-                device_id=wrapped(k),
+                recv_sem=mid_sem.at[r],
+                device_id=beside[i],
                 device_id_type=LOGICAL,
             ).start()
 
-    def wait_rows(ref, sem, r):
-        part = ref.at[r, pl.ds(0, tiles - 1)]
+    def wait_rows(ref, sem, r, own):
+        part = ref.at[r, pl.ds(own, tiles - own)]
         pltpu.make_async_copy(part, part, sem.at[r]).wait()
 
+    def pass_on(r):
+        wait_rows(mid_ref, mid_sem, r, planes)
+        for i in range(1, n_af):
+            recv_ref[r, i] = mid_ref[r, i * planes]
+        for j in range(1, planes):
+            for i in range(1, n_af):
+                pass_ref[r, j * n_af + i] = mid_ref[r, i * planes + j]
+        for j in range(1, planes):
+            pltpu.make_async_remote_copy(
+                src_ref=pass_ref.at[r, pl.ds(j * n_af, n_af)],
+                dst_ref=recv_ref.at[r, pl.ds((planes - j) * n_af, n_af)],
+                send_sem=pass_sem.at[r],
+                recv_sem=recv_sem.at[r],
+                device_id=across[j],
+                device_id_type=LOGICAL,
+            ).start()
+
     def take_all(r):
-        wait_rows(recv_ref, recv_sem, r)
+        wait_rows(recv_ref, recv_sem, r, n_af)
         return recv_ref[r][:, 0, :]
 
     def put_cross(r, field_ref, weights):
         rows = [jnp.broadcast_to(weights[i : i + 1, :], (8, 128)) for i in range(8)]
+        message = [None] * (tiles // 8)
         for q in range(half // 8):
             at_row = index_ref[0, 8 * q : 8 * q + 8]
             at_lane = index_ref[1, 8 * q : 8 * q + 8]
@@ -202,7 +237,8 @@
                 found = jnp.zeros((8, 128), f32)
                 for i in range(8):
                     found = jnp.where(at_row == i, taken(rows[i], at_lane), found)
-                put_eight(r, p, jnp.where(lane < SLOT, values, found))
+                message[p] = jnp.where(lane < SLOT, values, found)
+        put_rows(r, message)
 
     def take_cross(r):
         message = take_all(r)
@@ -224,8 +260,12 @@
             seg_values = jnp.where(of == t, taken(recv_ref[r, t], rank), seg_values)
         return [cells[8 * z : 8 * z + 8] for z in range(layers)], seg_values
 
-    owner = folded(loaded(8)[...]) - me
-    owner = jnp.where(owner < 0, owner + tiles, owner)
+    owner = folded(loaded(8)[...])
+    ahead = owner // n_af - plane
+    ahead = jnp.where(ahead < 0, ahead + planes, ahead)
+    along = owner % n_af - af
+    along = jnp.where(along < 0, along + n_af, along)
+    owner = ahead * n_af + along
     layer = folded(loaded(9)[...])
     cell = folded(loaded(10)[...])
     cell_row = (layer * width_x + cell // width_y).astype(f32) + 1.0
@@ -283,8 +323,7 @@
     pfrac_ref = loaded(3)
 
     pl.semaphore_wait(barrier, tiles - 1)
-    for q in (*range(half // 8, tiles // 8), *range(half // 8)):
-        put_eight(0, q, requests[8 * q : 8 * q + 8])
+    put_rows(0, by_eight(requests))
     start_halo(0)
     following = pltpu.make_async_remote_copy(
         src_ref=pfrac_ref,
@@ -295,6 +334,7 @@
         device_id_type=LOGICAL,
     )
     following.start()
+    pass_on(0)
 
     all_from, all_trans = loaded(12)[...], loaded(14)[...]
     from_hot = jnp.zeros((8, 128), f32)
@@ -343,8 +383,6 @@
         preferred_element_type=f32,
     )
     accum_ref = loaded(2)
-    put_halo(1, press, jnp.zeros((8, 128), f32))
-    start_halo(1)
 
     halo = take_halo(0)
     along_y = gy * n_af + af
@@ -382,6 +420,9 @@
     index_ref[1] = jnp.maximum(want_col, 0)
 
     put_cross(1, press_ref, coupling_mf * press_f)
+    put_halo(1, press, jnp.zeros((8, 128), f32))
+    start_halo(1)
+    pass_on(1)
     for j in range(half):
         at = slice(128 * j, 128 * j + 128)
         rows_ref[:, at] = hot(
@@ -428,6 +469,7 @@
         put_cross(r, adjm_ref, frac_ref[3] * frac)
         put_halo(r, field, jnp.broadcast_to(jnp.concatenate([sent, sent], axis=0), (8, 128)))
         start_halo(r)
+        pass_on(r)
         total = frac_ref[6] + chain(frac, frac_ref[0], frac_ref[1])
         for c in range(blocks):
             total = total + inter_ref[c] * sent[c : c + 1, :]
@@ -447,7 +489,8 @@
     following.wait_send()
 
     def finish(r, carry):
-        wait_rows(send_ref, send_sem, r)
+        wait_rows(send_ref, send_sem, r, planes)
+        wait_rows(pass_ref, pass_sem, r, n_af)
         for side in range(4):
             halo_copy(r, side).wait_send()
         return carry
@@ -469,7 +512,8 @@
     args = list(args)
     for i in range(11, 18):
         args[i] = args[i].reshape(1, -1)
-    tiles = sizes[0] * sizes[1] * sizes[2]
+    planes, n_af = sizes[0] * sizes[1], sizes[2]
+    tiles = planes * n_af
     layers, width_x, width_y = press_matrix.shape
     blocks, block_len = press_frac.shape
     slots = tiles * SLOT
@@ -495,11 +539,16 @@
             pltpu.VMEM((2, tiles, 128), jnp.int32),
             pltpu.VMEM((2, 8, 128), jnp.int32),
             pltpu.VMEM((ROUNDS, tiles, 1, 128), f32),
+            pltpu.VMEM((tiles, 1, 128), f32),
+            pltpu.VMEM((ROUNDS, tiles, 1, 128), f32),
+            pltpu.VMEM((ROUNDS, tiles, 1, 128), f32),
             pltpu.VMEM((ROUNDS, tiles, 1, 128), f32),
             pltpu.VMEM((ROUNDS, 4, 8, 128), f32),
             pltpu.VMEM((ROUNDS, 4, 8, 128), f32),
             pltpu.VMEM((blocks, block_len), f32),
             pltpu.SemaphoreType.DMA((18,)),
+            pltpu.SemaphoreType.DMA((ROUNDS,)),
+            pltpu.SemaphoreType.DMA((ROUNDS,)),
             pltpu.SemaphoreType.DMA((ROUNDS,)),
             pltpu.SemaphoreType.DMA((ROUNDS,)),
             pltpu.SemaphoreType.DMA((ROUNDS, 4)),

time: 54.7 us -> 73.7 us (1.35)
  Pallas kernels: 53.8 us -> 72.9 us
    pallas_call x1, Pallas kernels: 53.2 us -> 72.2 us  [body(): pl.pallas_call(functools.partial(kernel, sizes), out_shape=tuple((pltpu.V...]
where the time goes in v4:
time: 73.7 us; the launch traced here: 73.5 us
  Pallas kernels  72.9 us (99%)
    pallas_call x1, Pallas kernels, body(): pl.pallas_call(functools.partial(kernel, sizes), out_shape=tuple((pltpu.V...  72.2 us

profile of v4, /device:TPU:0, one launch (start us, length us, event | category | flops | bytes accessed | tf_op | source)
XLA Modules:
  0.0 73.5 jit_solution(10675211369502158114)
XLA Ops:
  0.6 72.2 %shard_map.201 = (f32[8,8,128]{2,1,0:T(8,128)S(1)}, f32[4,256]{1,0:T(4,128)S(1)}, f32[8,8,128]{2,1,0:T(8,128)S(1)}, f32[4,256]{1,0:T(4,128)S(1)}) custom-call(f32[8,8,128]{2,1,0:T(8,128)} %refs_0_.1, f32[8,8,128]{2,1,0:T(8,128)} %refs_1_.1, f32[8,8,128]{2,1,0:T(8,128)} %refs_2_.1, f32[4,256]{1,0:T(4,128)} %refs_3_.1, f32[4,256]{1,0:T(4,128)} %refs_4_.1, ...), custom_call_target="tpu_custom_call" | custom-call | tf_op jit(solution)/shard_map/pallas_call | solution.py:525
  72.9 0.7 shard_map.202
